TPU v7x, 128 devices: a whole 4x4x4 slice. The times are simulated.
128 devices in a mesh: row: 16 (over z, x), col: 8 (over y, core).
Axes of the slice: x: 4, y: 4, z: 4, core: 2. Of those that a mesh axis runs over, the one named last changes fastest.
Arguments:
- front: float32 [4, 4096, 8, 2048], P(None, 'row', None, 'col'), may hold values from -1 to 64, as said below
- child_blocks: float32 [1024, 256, 256], P(('row', 'col')), may hold values from -4 to 4
- child_rows: int32 [1024, 256], P(('row', 'col')), may hold values from 512 to 16383, as said below
- child_cols: int32 [1024, 256], P(('row', 'col')), may hold values from 512 to 16383, as said below
- child_count: int32 [128], P(('row', 'col')), may hold values from 5 to 8, as said below
Outputs:
- factored: float32 [4, 4096, 8, 2048], P(None, 'row', None, 'col')
Inputs may be any that keep to these rules, and one draw needn't show every extreme that they name: `front`: the first 512 diagonal entries lie in [32, 64]; every other entry lies in [-1, 1]. `child_rows`: all 256 rows of one child block land in one block row of index 2 or more whose index modulo 16 is the row index of the device that holds the block; positions within it may repeat. `child_cols`: all 256 columns of one child block land in one block column of index 2 or more; among the live blocks of one device at most 2 land in block columns of one device column (block column modulo 8), and on every device some device column gets exactly 2. `child_count`: some device has all 8 blocks live.
All inputs are finite; a program needn't handle non-finite values.
Results may differ from a plain program's by a relative error of at most 0.0001.
Values sent between devices are 32-bit elements; how exact they have to be, the bound alone decides.
A program may use at most 128 MiB of HBM per device.

v0:
```python
import jax
import jax.numpy as jnp
from jax import lax
from jax.sharding import PartitionSpec as P

CAP = 2
PANELS = 2


def spread(block, axis, source):
    block = jnp.where(lax.axis_index(axis) == source, block, jnp.zeros_like(block))
    return lax.psum(block, axis)


def local(front, child_blocks, child_rows, child_cols, child_count):
    blk_rows, block_size, blk_cols, _ = front.shape
    row_count = lax.axis_size("row")
    col_count = lax.axis_size("col")
    row_index = lax.axis_index("row")
    col_index = lax.axis_index("col")
    held_blocks = child_blocks.shape[0]
    owners = child_cols[:, 0] // block_size % col_count
    is_live = jnp.arange(held_blocks) < child_count[0]
    owner_match = owners[:, None] == jnp.arange(col_count)[None, :]
    col_hits = (owner_match & is_live[:, None]).astype(jnp.int32)
    earlier = jnp.cumsum(col_hits, axis=0) - col_hits
    block_rank = jnp.sum(earlier * owner_match.astype(jnp.int32), axis=1)
    slot_count = col_count * CAP
    target = jnp.where(is_live, owners * CAP + block_rank, slot_count)
    packed = (
        jnp.zeros((slot_count, block_size, block_size), jnp.float32)
        .at[target]
        .set(child_blocks, mode="drop")
    )
    packed_rows = (
        jnp.zeros((slot_count, block_size), jnp.int32).at[target].set(child_rows, mode="drop")
    )
    packed_cols = (
        jnp.zeros((slot_count, block_size), jnp.int32).at[target].set(child_cols, mode="drop")
    )
    received, received_rows, received_cols = (
        lax.all_to_all(
            packed.reshape(col_count, CAP, block_size, block_size),
            "col",
            split_axis=0,
            concat_axis=0,
            tiled=True,
        ),
        lax.all_to_all(
            packed_rows.reshape(col_count, CAP, block_size),
            "col",
            split_axis=0,
            concat_axis=0,
            tiled=True,
        ),
        lax.all_to_all(
            packed_cols.reshape(col_count, CAP, block_size),
            "col",
            split_axis=0,
            concat_axis=0,
            tiled=True,
        ),
    )
    received = received.reshape(slot_count, block_size, block_size)
    received_rows = received_rows.reshape(slot_count, block_size)
    received_cols = received_cols.reshape(slot_count, block_size)
    local_row = (received_rows[:, 0] // block_size // row_count).astype(jnp.int32)
    local_col = (received_cols[:, 0] // block_size // col_count).astype(jnp.int32)
    within_row = received_rows % block_size
    within_col = received_cols % block_size
    positions = jnp.arange(block_size, dtype=jnp.int32)

    def add_slot(slot, current):
        row_map = (within_row[slot][:, None] == positions[None, :]).astype(jnp.float32)
        col_map = (within_col[slot][:, None] == positions[None, :]).astype(jnp.float32)
        placed = jnp.dot(row_map.T, received[slot], precision=lax.Precision.HIGHEST)
        placed = jnp.dot(placed, col_map, precision=lax.Precision.HIGHEST)
        zero = jnp.int32(0)
        start = (local_row[slot], zero, local_col[slot], zero)
        old_block = lax.dynamic_slice(current, start, (1, block_size, 1, block_size))
        new_block = old_block + placed[None, :, None, :]
        return lax.dynamic_update_slice(current, new_block, start)

    front_work = lax.fori_loop(0, slot_count, add_slot, front)
    global_rows = jnp.arange(blk_rows) * row_count + row_index
    global_cols = jnp.arange(blk_cols) * col_count + col_index
    for panel in range(PANELS):
        panel_col = panel // col_count
        panel_row = panel // row_count
        col_owner = panel % col_count
        row_owner = panel % row_count
        column = front_work[:, :, panel_col, :]
        pivot_block = spread(column[panel_row], "row", row_owner)
        diag_factor = jnp.linalg.cholesky((pivot_block + pivot_block.T) * 0.5)
        solved = lax.linalg.triangular_solve(
            diag_factor,
            column.reshape(-1, block_size),
            left_side=False,
            lower=True,
            transpose_a=True,
        )
        solved = solved.reshape(blk_rows, block_size, block_size)
        lower_part = jnp.where(global_rows[:, None, None] > panel, solved, jnp.float32(0.0))
        panel_block = jnp.where(global_rows[:, None, None] == panel, diag_factor[None], lower_part)
        row_factor = spread(panel_block, "col", col_owner)
        gathered = lax.all_gather(row_factor[:, None], "row", axis=1, tiled=True)
        gathered = gathered.reshape(blk_cols, col_count, block_size, block_size)
        col_factor = lax.dynamic_index_in_dim(gathered, col_index, 1, keepdims=False)
        left_part = jnp.where(global_rows[:, None, None] > panel, row_factor, jnp.float32(0.0))
        right_part = jnp.where(global_cols[:, None, None] > panel, col_factor, jnp.float32(0.0))
        update = jnp.einsum("aps,bqs->apbq", left_part, right_part, precision=lax.Precision.HIGHEST)
        front_work = front_work - update
        new_column = jnp.where(col_index == col_owner, row_factor, front_work[:, :, panel_col, :])
        front_work = front_work.at[:, :, panel_col, :].set(new_column)
        wipe_mask = (global_rows == panel)[:, None, None, None] & (global_cols > panel)[
            None, None, :, None
        ]
        front_work = jnp.where(wipe_mask, jnp.float32(0.0), front_work)
    return front_work


def solution(mesh):
    placed = (
        P(None, "row", None, "col"),
        P(("row", "col"), None, None),
        P(("row", "col"), None),
        P(("row", "col"), None),
        P(("row", "col")),
    )
    return jax.shard_map(
        local, mesh=mesh, in_specs=placed, out_specs=P(None, "row", None, "col"), check_vma=False
    )
```

profile of v0, /device:TPU:11, one launch (start us, length us, event | category | flops | bytes accessed | tf_op | source)
XLA Modules:
  0.0 918.1 jit_solution(11119409476042689646)
XLA Ops:
  9.7 5.2 all-to-all-start.1
  16.3 2.1 all-to-all-done.1
  18.5 5.1 all-to-all-start
  23.5 2.4 broadcast_in_dim.137
  26.0 4.3 scatter_fusion
  30.2 4.8 all-to-all-start.2
  35.0 9.3 %copy.35 = f32[4,256,8,256]{3,1,2,0:T(8,128)} copy(f32[4,256,8,256]{3,2,1,0:T(8,128)} %param.14) | data formatting | bytes 16777216
  44.7 38.1 %all-to-all-done.2 = f32[8,2,256,256]{3,2,1,0:T(8,128)} async-done(((f32[8,2,256,256]{3,2,1,0:T(8,128)}), f32[8,2,256,256]{3,2,1,0:T(8,128)}, u32[]{:S(2)}, u32[]{:S(2)}) %all-to-all-start.2) | async-done | bytes 4194336 | tf_op jit(solution)/shard_map/all_to_all | solution.py:42
  82.8 133.7 %while.21 = (s32[]{:T(128)}, f32[4,256,8,256]{3,1,2,0:T(8,128)}, s32[16]{0:T(128)S(1)}, s32[16]{0:T(128)S(1)}, s32[16,256]{1,0:T(8,128)S(1)}, /*index=5*/f32[16,...) while((s32[]{:T(128)}, f32[4,256,8,256]{3,1,2,0:T(8,128)}, ...), condition=%wide.region_6.7_spmd.clone.clone, body=%wide.region_5.6_spmd.clone.clone.sunk | while | flops 402849792 | bytes 1317589 | solution.py:84
  114.2 2.0 fusion.89
  122.6 2.0 fusion.89
  139.3 2.0 fusion.89
  219.8 82.2 %all-reduce.6.cloned.1.call-done = f32[256,256]{1,0:T(8,128)} async-done(((f32[256,256]{1,0:T(8,128)}), f32[256,256]{1,0:T(8,128)}) %all-reduce.6.cloned.1.call-update) | async-done | bytes 262160 | tf_op jit(solution)/shard_map/psum | solution.py:12
  304.3 11.7 %cholesky.130 = f32[128,128]{1,0:T(8,128)S(1)} custom-call(f32[128,128]{1,0:T(8,128)S(1)} %cholesky.194), custom_call_target="Cholesky" | custom-call | tf_op jit(solution)/shard_map/jit(cholesky)/cholesky | solution.py:94
  316.1 9.8 %custom-call.13 = f32[1,128,128]{1,2,0:T(8,128)S(1)} custom-call(f32[1,128,128]{2,1,0:T(8,128)S(1)} %get-tuple-element.294), custom_call_target="InvertDiagBlocksLowerTriangular" | custom-call | tf_op jit(solution)/shard_map/jit(cholesky)/cholesky | solution.py:94
  326.3 11.7 %cholesky.147 = f32[128,128]{1,0:T(8,128)S(1)} custom-call(f32[128,128]{1,0:T(8,128)S(1)} %convolution_subtract_fusion.4), custom_call_target="Cholesky" | custom-call | tf_op jit(solution)/shard_map/jit(cholesky)/cholesky | solution.py:94
  340.2 4.3 while.22
  344.5 19.7 %custom-call.14 = f32[2,128,128]{1,2,0:T(8,128)S(1)} custom-call(f32[2,128,128]{2,1,0:T(8,128)S(1)} %get-tuple-element.224), custom_call_target="InvertDiagBlocksLowerTriangular" | custom-call | tf_op jit(solution)/shard_map/triangular_solve/custom-call.0 | solution.py:95
  368.2 59.9 %all-reduce.8.cloned.1.call-done = f32[4,256,256]{2,1,0:T(8,128)} async-done(((f32[4,256,256]{2,1,0:T(8,128)}), f32[4,256,256]{2,1,0:T(8,128)}) %all-reduce.8.cloned.1.call-update) | async-done | bytes 1048592 | tf_op jit(solution)/shard_map/psum | solution.py:12
  428.2 117.1 %all-gather.5.cloned.1.call-done = f32[4,4096,256]{2,1,0:T(8,128)} async-done(((f32[4,256,256]{2,1,0:T(8,128)}), f32[4,4096,256]{2,1,0:T(8,128)}) %all-gather.5.cloned.1.call-update) | async-done | bytes 16777232 | tf_op jit(solution)/shard_map/all_gather | solution.py:106
  545.4 12.1 %copy_subtract_fusion = f32[4,256,8,256]{3,1,0,2:T(8,128)S(1)} fusion(f32[4,256,8,256]{3,1,2,0:T(8,128)} %get-tuple-element.173, f32[8,8,256,256]{3,2,1,0:T(8,128)} %bitcast.184, s32[]{:T(128)S(6)} %select_n.178, f32[4,256,256]{2,1,0:T(8,128)} %all-reduce.8.cloned.1.call-done, pred[8]{0:T(512)(128)(4,1)S(1)} %fusion.64, pred[4]{0:T(512)(128)(4,1)S(1)} %get-tuple-element.299), kind=kOutput, calls=%fused_computation.22 | convolution fusion | flops 6445334528 | bytes 19922960 | tf_op jit(solution)/shard_map/aps,bqs->apbq/dot_general | solution.py:111
  559.0 3.4 copy-done
  564.9 80.2 %all-reduce.10.cloned.1.call-done = f32[256,256]{1,0:T(8,128)} async-done(((f32[256,256]{1,0:T(8,128)}), f32[256,256]{1,0:T(8,128)}) %all-reduce.10.cloned.1.call-update) | async-done | bytes 262160 | tf_op jit(solution)/shard_map/psum | solution.py:12
  647.5 11.7 %cholesky.164 = f32[128,128]{1,0:T(8,128)S(1)} custom-call(f32[128,128]{1,0:T(8,128)S(1)} %cholesky.197), custom_call_target="Cholesky" | custom-call | tf_op jit(solution)/shard_map/jit(cholesky)/cholesky | solution.py:94
  659.3 9.8 %custom-call.15 = f32[1,128,128]{1,2,0:T(8,128)S(1)} custom-call(f32[1,128,128]{2,1,0:T(8,128)S(1)} %get-tuple-element.290), custom_call_target="InvertDiagBlocksLowerTriangular" | custom-call | tf_op jit(solution)/shard_map/jit(cholesky)/cholesky | solution.py:94
  669.6 11.7 %cholesky.181 = f32[128,128]{1,0:T(8,128)S(1)} custom-call(f32[128,128]{1,0:T(8,128)S(1)} %convolution_subtract_fusion.3), custom_call_target="Cholesky" | custom-call | tf_op jit(solution)/shard_map/jit(cholesky)/cholesky | solution.py:94
  684.0 4.2 while.23
  688.3 19.7 %custom-call.16 = f32[2,128,128]{1,2,0:T(8,128)S(1)} custom-call(f32[2,128,128]{2,1,0:T(8,128)S(1)} %get-tuple-element.225), custom_call_target="InvertDiagBlocksLowerTriangular" | custom-call | tf_op jit(solution)/shard_map/triangular_solve/custom-call.0 | solution.py:95
  711.9 59.9 %all-reduce.12.cloned.1.call-done = f32[4,256,256]{2,1,0:T(8,128)} async-done(((f32[4,256,256]{2,1,0:T(8,128)}), f32[4,256,256]{2,1,0:T(8,128)}) %all-reduce.12.cloned.1.call-update) | async-done | bytes 1048592 | tf_op jit(solution)/shard_map/psum | solution.py:12
  771.9 116.8 %all-gather.7.cloned.1.call-done = f32[4,4096,256]{2,1,0:T(8,128)} async-done(((f32[4,256,256]{2,1,0:T(8,128)}), f32[4,4096,256]{2,1,0:T(8,128)}) %all-gather.7.cloned.1.call-update) | async-done | bytes 16777232 | tf_op jit(solution)/shard_map/all_gather | solution.py:106
  888.7 12.6 %convolution_subtract_fusion = f32[4,256,8,256]{3,1,2,0:T(8,128)S(1)} fusion(f32[4,256,8,256]{3,1,2,0:T(8,128)} %copy-done, f32[8,8,256,256]{3,2,1,0:T(8,128)} %bitcast.185, s32[]{:T(128)S(6)} %select_n.178, f32[4,256,256]{2,1,0:T(8,128)} %all-reduce.12.cloned.1.call-done, pred[8]{0:T(512)(128)(4,1)S(1)} %fusion.65, pred[4]{0:T(512)(128)(4,1)S(1)} %get-tuple-element.301), kind=kOutput, calls=%fused_computation.24 | convolution fusion | flops 6445334528 | bytes 19922960 | tf_op jit(solution)/shard_map/aps,bqs->apbq/dot_general | solution.py:111
  902.8 8.3 copy.47
  (184 shorter events, 105.0 us)
Async XLA Ops:
  9.7 8.8 all-to-all-start.1
  18.5 11.7 %all-to-all-start = ((s32[8,2,256]{2,1,0:T(2,128)}), s32[8,2,256]{2,1,0:T(2,128)S(1)}, u32[]{:S(2)}, u32[]{:S(2)}) async-start(s32[8,2,256]{2,1,0:T(2,128)} %reshape.258), calls=%async_computation | async-start | bytes 32768 | tf_op jit(solution)/shard_map/all_to_all | solution.py:49
  30.2 52.6 %all-to-all-start.2 = ((f32[8,2,256,256]{3,2,1,0:T(8,128)}), f32[8,2,256,256]{3,2,1,0:T(8,128)}, u32[]{:S(2)}, u32[]{:S(2)}) async-start(f32[8,2,256,256]{3,2,1,0:T(8,128)} %bitcast.175), calls=%async_computation.2 | async-start | bytes 8388608 | tf_op jit(solution)/shard_map/all_to_all | solution.py:42
  35.0 267.0 %all-reduce.6.cloned.1.call-start = ((), (), s32[]{:S(2)}) async-start(), calls=%async_computation.3 | async-start | bytes 524288 | tf_op jit(solution)/shard_map/psum | solution.py:12
  218.2 209.8 %all-reduce.8.cloned.1.call-start = ((), (), s32[]{:S(2)}) async-start(), calls=%async_computation.4 | async-start | bytes 2097152 | tf_op jit(solution)/shard_map/psum | solution.py:12
  368.1 177.2 %all-gather.5.cloned.1.call-start = ((), (), s32[]{:S(2)}) async-start(), calls=%async_computation.7 | async-start | bytes 17825792 | tf_op jit(solution)/shard_map/all_gather | solution.py:106
  428.1 217.0 %all-reduce.10.cloned.1.call-start = ((), (), s32[]{:S(2)}) async-start(), calls=%async_computation.5 | async-start | bytes 524288 | tf_op jit(solution)/shard_map/psum | solution.py:12
  545.4 12.2 %copy-start.1 = (f32[4,256,256]{2,1,0:T(8,128)S(1)}, f32[4,256,256]{2,1,0:T(8,128)}, u32[]{:S(2)}) copy-start(f32[4,256,256]{2,1,0:T(8,128)} %all-reduce.8.cloned.1.call-done) | copy-start | bytes 3145732
  559.0 3.4 copy-start
  563.1 208.7 %all-reduce.12.cloned.1.call-start = ((), (), s32[]{:S(2)}) async-start(), calls=%async_computation.6 | async-start | bytes 2097152 | tf_op jit(solution)/shard_map/psum | solution.py:12
  711.9 176.9 %all-gather.7.cloned.1.call-start = ((), (), s32[]{:S(2)}) async-start(), calls=%async_computation.8 | async-start | bytes 17825792 | tf_op jit(solution)/shard_map/all_gather | solution.py:106
  888.7 12.6 %copy-start.2 = (f32[4,256,256]{2,1,0:T(8,128)S(1)}, f32[4,256,256]{2,1,0:T(8,128)}, u32[]{:S(2)}) copy-start(f32[4,256,256]{2,1,0:T(8,128)} %all-reduce.12.cloned.1.call-done) | copy-start | bytes 3145732
Sparse Core Ops, SparseCore 0:
  218.3 83.6 all-reduce.5
  368.2 59.7 all-reduce.7
  430.4 114.8 all-gather.4
  563.3 81.7 all-reduce.9
  712.0 59.7 all-reduce.11
  773.8 114.8 all-gather.6
where the time goes:
time: 926 us; the launch traced here: 918 us
  waiting for transfers between devices  556 us (60%)
  other arithmetic  119 us (13%)
  matrix products  85.1 us (9%)
  local copies, waits for them, and re-layouts  64.7 us (7%)
  loops' own time  60.1 us (6%)
  between operations  17.3 us (2%)
  starting transfers between devices  15.8 us (2%)
    psum x4, waiting for transfers between devices, spread(): return lax.psum(block, axis)  282 us
    all_gather x2, waiting for transfers between devices, local(): gathered = lax.all_gather(row_factor[:, None], 'row', axis=1, tiled=True)  234 us
    another operation x13, other arithmetic, local(): diag_factor = jnp.linalg.cholesky((pivot_block + pivot_block.T) * 0.5)  68.7 us
    another operation x1, loops' own time, local(): front_work = lax.fori_loop(0, slot_count, add_slot, front)  59.6 us
    another operation x7, other arithmetic, local(): lax.linalg.triangular_solve(diag_factor, column.reshape(-1, block_size),...  39.6 us
    all_to_all x1, waiting for transfers between devices, local(): lax.all_to_all(packed.reshape(col_count, CAP, block_size, block_size), 'c...  38.1 us
    dot_general x16, matrix products, add_slot(): placed = jnp.dot(placed, col_map, precision=lax.Precision.HIGHEST)  32.3 us
    dot_general x2, matrix products, local(): jnp.einsum('aps,bqs->apbq', left_part, right_part, precision=lax.Precisio...  24.7 us
  transfers between devices with their start and end apart: 9, of which 8 were waited for; matrix products, arithmetic and copies ran while one was open for 2% of the time, Pallas kernels for 0%

commit v1 on v0

v1 whole, which is shorter than its diff:
```python
import functools

import jax
import jax.numpy as jnp
from jax import lax
from jax.experimental import pallas as pl
from jax.experimental.pallas import tpu as pltpu
from jax.sharding import PartitionSpec as P

F32 = jnp.float32
BF = jnp.bfloat16
MESH = pl.DeviceIdType.MESH
TN = (((0,), (0,)), ((), ()))
NT = (((1,), (1,)), ((), ()))
NN = (((1,), (0,)), ((), ()))


def hdot(a, b, dn):
    return lax.dot_general(a, b, dn, precision=lax.Precision.HIGHEST, preferred_element_type=F32)


def bdot(a, b, dn):
    return lax.dot_general(a, b, dn, preferred_element_type=F32)


def split(x):
    hi = x.astype(BF)
    return hi, (x - hi.astype(F32)).astype(BF)


def factor(A, group=8, strip=32):
    ns = 128//strip
    lane = lax.broadcasted_iota(jnp.int32,(strip,128),1)
    sub = lax.broadcasted_iota(jnp.int32,(strip,128),0)
    def tile(J,carry):
        c0 = pl.multiple_of(J*128,128)
        for t in range(ns):
            r0 = pl.multiple_of(c0+strip*t,strip)
            S = [A[pl.ds(r0,strip),128*i:128*i+128] for i in range(4)]
            T = A[pl.ds(r0,strip),pl.ds(c0,128)]
            for s0 in range(0,strip,group):
                cols=[jnp.broadcast_to(T[:,strip*t+s0+a:strip*t+s0+a+1],(strip,128)) for a in range(group)]
                fs=[]
                for a in range(group):
                    s=s0+a
                    rd=1.0/cols[a][s:s+1,:]
                    f=jnp.where(sub>s,cols[a]*rd,0.0)
                    fs.append(f)
                    for b in range(a+1,group):
                        cols[b]=cols[b]-f*cols[b][s:s+1,:]
                for a in range(group):
                    s=s0+a; k=strip*t+s
                    f=fs[a]
                    rowT=jnp.where(lane[:1]==k,1.0,T[s:s+1,:])
                    T=jnp.where((lane==k)&(sub>s),0.0,T)-f*rowT
                    S=[x-f*x[s:s+1,:] for x in S]
            dg=(lane==sub+strip*t)
            d=jnp.sum(jnp.where(dg,T,0.0),axis=1,keepdims=True)
            rs=lax.rsqrt(d)
            rs=rs*(1.5-0.5*d*rs*rs)
            rs=jnp.broadcast_to(rs,(strip,128))
            T=jnp.where(dg,1.0,T)*rs
            for i in range(4): A[pl.ds(r0,strip),128*i:128*i+128]=S[i]*rs
            if t<ns-1:
                n=128-strip*(t+1)
                A[pl.ds(r0,strip),pl.ds(c0,128)]=jnp.where((lane>sub+strip*t)&(lane<strip*(t+1)),0.0,T)
                R=A[pl.ds(r0,strip),:]
                lm=jnp.where(lane>=strip*(t+1),T,0.0)
                upd=hdot(lm,R,TN)
                rb=pl.multiple_of(r0+strip,strip)
                lane_n=lax.broadcasted_iota(jnp.int32,(n,128),1)
                Tt=A[pl.ds(rb,n),pl.ds(c0,128)]
                A[pl.ds(rb,n),pl.ds(c0,128)]=jnp.where((lane_n>=strip*t)&(lane_n<strip*(t+1)),0.0,Tt)
                A[pl.ds(rb,n),:]=A[pl.ds(rb,n),:]-upd[strip*(t+1):]
            A[pl.ds(r0,strip),pl.ds(c0,128)]=T
        R=A[pl.ds(c0,128),:]
        D=A[pl.ds(c0,128),pl.ds(c0,128)]
        i1=lax.broadcasted_iota(jnp.int32,(128,128),1); i0=lax.broadcasted_iota(jnp.int32,(128,128),0)
        D=jnp.where(i1>i0,0.0,D)
        for m in range(1,4):
            @pl.when(m>J)
            def _(m=m):
                lm=A[pl.ds(c0,128),m*128:(m+1)*128]
                A[m*128:(m+1)*128,:]=A[m*128:(m+1)*128,:]-hdot(lm,R,TN)
                A[m*128:(m+1)*128,pl.ds(c0,128)]=-hdot(lm,D,TN)
        return carry
    lax.fori_loop(0,4,tile,0)


def m4(v):
    return lax.rem(v + 8, 4)


def comm_kernel(
    pan, cb, crow, ccol, crow_s, ccol_s, cnt_s,
    recv, lrh, lrl, lch, lcl, corner,
    stage, PR, PC, DG, AW, Wh, Wl, oh, ol,
    h0, h1, h2, h3, h4, h5, y0s, y0r, y1s, y1r, ds, dr, dloc, xs_, xr_, cs, cr, osem,
):
    r = lax.axis_index("row")
    c = lax.axis_index("col")
    z, x = r // 4, lax.rem(r, 4)
    y, k = c // 2, lax.rem(c, 2)

    def dev(z, x, y, k):
        return (z * 4 + x, y * 2 + k)

    other = dev(z, x, y, 1 - k)
    b = pltpu.get_barrier_semaphore()
    for d in range(1, 8):
        pl.semaphore_signal(b, inc=1, device_id=(r, lax.rem(c + d, 8)), device_id_type=MESH)
    for s in (1, 3):
        pl.semaphore_signal(b, inc=1, device_id=dev(z, m4(x + s), y, k), device_id_type=MESH)
        pl.semaphore_signal(b, inc=1, device_id=dev(m4(z + s), x, y, k), device_id_type=MESH)
    pl.semaphore_wait(b, 11)

    def rcopy(src, dst, ss, rs, to):
        return pltpu.make_async_remote_copy(
            src_ref=src, dst_ref=dst, send_sem=ss, recv_sem=rs, device_id=to, device_id_type=MESH
        )

    def pack():
        owner = [lax.rem(ccol_s[s, 0] // 256, 8) for s in range(8)]
        live = [(s < cnt_s[0]).astype(jnp.int32) for s in range(8)]
        rank = []
        for s in range(8):
            n = jnp.int32(0)
            for q in range(s):
                n = n + live[q] * (owner[q] == owner[s]).astype(jnp.int32)
            rank.append(n)

        def slot(t, carry):
            idx = jnp.int32(0)
            ok = jnp.int32(0)
            for s in range(8):
                hit = live[s] * (owner[s] * 2 + rank[s] == t).astype(jnp.int32)
                idx = idx + hit * s
                ok = ok + hit
            rows = crow[pl.ds(idx, 1), :]
            cols = ccol[pl.ds(idx, 1), :]
            brow = rows // 4096
            bcol = cols // 2048
            code = jnp.where(ok > 0, brow * 8 + bcol, -1)
            stage[t, 0:256, :] = cb[idx]
            stage[t, 256:257, :] = lax.rem(rows, 256).astype(F32)
            stage[t, 257:258, :] = lax.rem(cols, 256).astype(F32)
            stage[t, 258:259, :] = code.astype(F32)
            stage[t, 259:264, :] = jnp.zeros((5, 256), F32)
            return carry

        lax.fori_loop(0, 16, slot, 0)

    def child_copy(d):
        to = lax.rem(c + d, 8)
        return rcopy(
            stage.at[pl.ds(to * 2, 2)], recv.at[pl.ds(c * 2, 2)], cs.at[d], cr.at[d], (r, to)
        )

    own_copy = pltpu.make_async_copy(stage.at[pl.ds(c * 2, 2)], recv.at[pl.ds(c * 2, 2)], cs.at[0])

    def start_children():
        own_copy.start()
        for d in (1, 7, 2, 6, 3, 5, 4):
            child_copy(d).start()

    def wait_children():
        own_copy.wait()
        for d in range(1, 8):
            child_copy(d).wait()

    def tree(src_z, src_x, xfirst, s1, s2, make):
        oz, ox = z - src_z, x - src_x
        a = m4(s1 * jnp.where(xfirst == 1, ox, oz))
        bb = m4(s2 * jnp.where(xfirst == 1, oz, ox))
        dz1, dx1 = jnp.where(xfirst == 1, 0, s1), jnp.where(xfirst == 1, s1, 0)
        dz2, dx2 = jnp.where(xfirst == 1, s2, 0), jnp.where(xfirst == 1, 0, s2)
        is_src = jnp.logical_and(a == 0, bb == 0)
        conds = (
            jnp.logical_and(bb == 0, a <= 1),
            jnp.logical_and(bb == 0, a == 0),
            bb <= 1,
            bb == 0,
        )
        targets = (
            dev(m4(z + dz1), m4(x + dx1), y, k),
            dev(m4(z - dz1), m4(x - dx1), y, k),
            dev(m4(z + dz2), m4(x + dx2), y, k),
            dev(m4(z - dz2), m4(x - dx2), y, k),
        )
        copies = [make(e, to) for e, to in enumerate(targets)]
        return is_src, conds, copies

    h0_copy = rcopy(pan.at[pl.ds(1, 3)], PR.at[0, pl.ds(1, 3)], h0.at[0], h0.at[1], other)
    h1_copy = rcopy(pan.at[0], PR.at[1, 0], h1.at[0], h1.at[1], other)
    h2_copy = [
        rcopy(PR.at[p, 0], PR.at[p, 0], h2.at[p, 0], h2.at[p, 1], other) for p in range(2)
    ]
    h3_copy = rcopy(AW, AW, h3.at[0], h3.at[1], other)

    def h4_copy(j):
        p, br = lax.rem(j, 2), 1 + j // 2
        return rcopy(PR.at[p, br], PR.at[p, br], h4.at[j, 0], h4.at[j, 1], other)

    def xz_index(q):
        i, s = q // 4, lax.rem(q, 4)
        return lax.rem(s, 2), s // 2, lax.rem(i, 2), lax.rem(i // 2 + 1, 4)

    def h5_copy(q):
        kk, src, p, br = xz_index(q)
        ref = PC.at[kk, src, p, br]
        return rcopy(ref, ref, h5.at[q, 0], h5.at[q, 1], other)

    def y0_parts(j):
        p, qt = j // 4, lax.rem(j, 4)
        s = 1 - 2 * p
        yy = m4(s * y)
        ref = PR.at[p, 0, pl.ds(qt * 64, 64)]
        fwd = rcopy(ref, ref, y0s.at[j, 0], y0r.at[j], dev(z, x, m4(y + s), k))
        back = rcopy(ref, ref, y0s.at[j, 1], y0r.at[j], dev(z, x, m4(y - s), k))
        return yy, fwd, back

    def d_parts(j):
        d, qt = j // 4, lax.rem(j, 4)
        rows = pl.ds(qt * 64, 64)
        ref = DG.at[d, rows]
        src_x = jnp.minimum(d, 1)
        s1 = 1 - 2 * lax.rem(d, 2)
        parts = tree(
            0, src_x, 1, s1, s1, lambda e, to: rcopy(ref, ref, ds.at[j, e], dr.at[j], to)
        )
        return parts, d, rows

    @pl.when(k == 0)
    def _():
        @pl.when(y == 0)
        def _():
            h0_copy.start()
            PR[0, 0] = pan[0]

        def y0_step(j, carry):
            yy, fwd, back = y0_parts(j)

            @pl.when(yy != 0)
            def _():
                fwd.wait_recv()

            @pl.when(jnp.logical_and(yy == 0, j == 4))
            def _():
                h1_copy.wait_recv()

            @pl.when(yy <= 1)
            def _():
                fwd.start()

            @pl.when(yy == 0)
            def _():
                back.start()

            return carry

        lax.fori_loop(0, 8, y0_step, 0)
        for p in range(2):
            h2_copy[p].start()

        def d_step(j, carry):
            (is_src, conds, copies), d, rows = d_parts(j)

            @pl.when(is_src)
            def _():
                DG[d, rows, :] = PR[d // 2, 0, rows, :]

            @pl.when(jnp.logical_not(is_src))
            def _():
                copies[0].wait_recv()

            for cond, cp in zip(conds, copies):
                @pl.when(cond)
                def _(cp=cp):
                    cp.start()

            return carry

        lax.fori_loop(0, 12, d_step, 0)
        pack()
        start_children()

        AW[0:256, 0:256] = (DG[0] + DG[0].T) * 0.5
        AW[0:256, 256:512] = DG[1].T
        AW[256:512, 0:256] = jnp.zeros((256, 256), F32)
        AW[256:512, 256:512] = (DG[2] + DG[2].T) * 0.5
        factor(AW)
        h3_copy.start()

        def h4_wait(j, carry):
            h4_copy(j).wait_recv()
            return carry

        lax.fori_loop(0, 6, h4_wait, 0)

        def h5_wait(q, carry):
            @pl.when(lax.rem(q, 2) == 0)
            def _():
                h5_copy(q).wait_recv()

            return carry

        lax.fori_loop(0, 32, h5_wait, 0)

    def y1_parts(j):
        p, br = lax.rem(j, 2), 1 + j // 2
        s = 1 - 2 * p
        yy = m4(s * y)
        ref = PR.at[p, br]
        return yy, rcopy(ref, ref, y1s.at[j], y1r.at[j], dev(z, x, m4(y + s), k))

    def xz_parts(q):
        kk, src, p, br = xz_index(q)
        i = q // 4
        row = 2 * y + kk + 8 * src
        ref = PC.at[kk, src, p, br]
        xfirst = lax.rem(i, 2)
        s1 = 1 - 2 * lax.rem(i // 2, 2)
        s2 = 1 - 2 * lax.rem(i // 4, 2)
        return tree(
            row // 4, lax.rem(row, 4), xfirst, s1, s2,
            lambda e, to: rcopy(ref, ref, xs_.at[q, e], xr_.at[q], to),
        )

    @pl.when(k == 1)
    def _():
        @pl.when(y == 0)
        def _():
            PR[1, 1:4] = pan[1:4]
            h1_copy.start()
            h0_copy.wait_recv()

        def y1_step(j, carry):
            yy, fwd = y1_parts(j)

            @pl.when(yy != 0)
            def _():
                fwd.wait_recv()

            @pl.when(yy < 3)
            def _():
                fwd.start()

            h4_copy(j).start()
            return carry

        lax.fori_loop(0, 6, y1_step, 0)
        pack()
        start_children()
        for p in range(2):
            h2_copy[p].wait_recv()

        def xz_step(q, carry):
            is_src, conds, copies = xz_parts(q)
            kk, src, p, br = xz_index(q)

            @pl.when(is_src)
            def _():
                PC[kk, src, p, br] = PR[p, br]

            @pl.when(jnp.logical_not(is_src))
            def _():
                copies[0].wait_recv()

            for cond, cp in zip(conds, copies):
                @pl.when(cond)
                def _(cp=cp):
                    cp.start()

            @pl.when(kk == 0)
            def _():
                h5_copy(q).start()

            return carry

        lax.fori_loop(0, 32, xz_step, 0)
        h3_copy.wait_recv()

    i0 = lax.broadcasted_iota(jnp.int32, (256, 256), 0)
    i1 = lax.broadcasted_iota(jnp.int32, (256, 256), 1)
    low = i1 <= i0
    Wh[0], Wl[0] = split(jnp.where(low, AW[0:256, 0:256], 0.0))
    Wh[1], Wl[1] = split(AW[256:512, 0:256])
    Wh[2], Wl[2] = split(jnp.where(low, AW[256:512, 256:512], 0.0))

    def times_w(h, l, w):
        return bdot(h, Wh[w], NT) + (bdot(h, Wl[w], NT) + bdot(l, Wh[w], NT))

    def solve(m0, m1, put):
        h0_, l0_ = split(m0)
        h1_, l1_ = split(m1)
        a = times_w(h0_, l0_, 0)
        put(0, *split(a))
        e = times_w(h0_, l0_, 1) + times_w(h1_, l1_, 2)
        put(1, *split(e))

    def row_solve(i, carry):
        def put(p, hi, lo):
            oh[i, :, pl.ds(p * 256, 256)] = hi
            ol[i, :, pl.ds(p * 256, 256)] = lo

        solve(PR[0, i], PR[1, i], put)
        return carry

    lax.fori_loop(0, 4, row_solve, 0)

    def col_solve(i, carry):
        def put(p, hi, lo):
            oh[4 + i, :, pl.ds(p * 256, 256)] = hi
            ol[4 + i, :, pl.ds(p * 256, 256)] = lo

        solve(PC[k, lax.rem(i, 2), 0, i // 2], PC[k, lax.rem(i, 2), 1, i // 2], put)
        return carry

    lax.fori_loop(0, 8, col_solve, 0)
    outs = [
        pltpu.make_async_copy(oh.at[pl.ds(0, 4)], lrh, osem.at[0]),
        pltpu.make_async_copy(ol.at[pl.ds(0, 4)], lrl, osem.at[1]),
        pltpu.make_async_copy(oh.at[pl.ds(4, 8)], lch, osem.at[2]),
        pltpu.make_async_copy(ol.at[pl.ds(4, 8)], lcl, osem.at[3]),
    ]
    for cp in outs:
        cp.start()

    corner[...] = jnp.zeros((256, 256), F32)

    def diag_block(o):
        t = AW[o : o + 256, o : o + 256].T
        return jnp.where(i1 < i0, t, jnp.where(i1 == i0, 1.0 / t, 0.0))

    @pl.when(jnp.logical_and(r == 0, c == 0))
    def _():
        corner[...] = diag_block(0)

    @pl.when(jnp.logical_and(r == 1, c == 0))
    def _():
        corner[...] = AW[0:256, 256:512].T

    @pl.when(jnp.logical_and(r == 1, c == 1))
    def _():
        corner[...] = diag_block(256)

    @pl.when(k == 0)
    def _():
        @pl.when(y == 0)
        def _():
            h0_copy.wait_send()

        def y0_end(j, carry):
            yy, fwd, back = y0_parts(j)

            @pl.when(yy <= 1)
            def _():
                fwd.wait_send()

            @pl.when(yy == 0)
            def _():
                back.wait_send()

            return carry

        lax.fori_loop(0, 8, y0_end, 0)
        for p in range(2):
            h2_copy[p].wait_send()

        def d_end(j, carry):
            (is_src, conds, copies), d, rows = d_parts(j)
            for cond, cp in zip(conds, copies):
                @pl.when(cond)
                def _(cp=cp):
                    cp.wait_send()

            return carry

        lax.fori_loop(0, 12, d_end, 0)
        h3_copy.wait_send()

    @pl.when(k == 1)
    def _():
        @pl.when(y == 0)
        def _():
            h1_copy.wait_send()

        def y1_end(j, carry):
            yy, fwd = y1_parts(j)

            @pl.when(yy < 3)
            def _():
                fwd.wait_send()

            h4_copy(j).wait_send()
            return carry

        lax.fori_loop(0, 6, y1_end, 0)

        def xz_end(q, carry):
            is_src, conds, copies = xz_parts(q)
            for cond, cp in zip(conds, copies):
                @pl.when(cond)
                def _(cp=cp):
                    cp.wait_send()

            @pl.when(lax.rem(q, 2) == 0)
            def _():
                h5_copy(q).wait_send()

            return carry

        lax.fori_loop(0, 32, xz_end, 0)

    wait_children()
    for cp in outs:
        cp.wait()


def exchange(pan, child_blocks, child_rows, child_cols, child_count):
    vm = pl.BlockSpec(memory_space=pltpu.VMEM)
    sm = pl.BlockSpec(memory_space=pltpu.SMEM)
    hbm = pl.BlockSpec(memory_space=pl.ANY)
    dma = pltpu.SemaphoreType.DMA
    return pl.pallas_call(
        comm_kernel,
        out_shape=(
            jax.ShapeDtypeStruct((16, 264, 256), F32),
            jax.ShapeDtypeStruct((4, 256, 512), BF),
            jax.ShapeDtypeStruct((4, 256, 512), BF),
            jax.ShapeDtypeStruct((8, 256, 512), BF),
            jax.ShapeDtypeStruct((8, 256, 512), BF),
            jax.ShapeDtypeStruct((256, 256), F32),
        ),
        in_specs=[vm, vm, vm, vm, sm, sm, sm],
        out_specs=(hbm, hbm, hbm, hbm, hbm, vm),
        scratch_shapes=[
            pltpu.VMEM((16, 264, 256), F32),
            pltpu.VMEM((2, 4, 256, 256), F32),
            pltpu.VMEM((2, 2, 2, 4, 256, 256), F32),
            pltpu.VMEM((3, 256, 256), F32),
            pltpu.VMEM((512, 512), F32),
            pltpu.VMEM((3, 256, 256), BF),
            pltpu.VMEM((3, 256, 256), BF),
            pltpu.VMEM((12, 256, 512), BF),
            pltpu.VMEM((12, 256, 512), BF),
            dma((2,)), dma((2,)), dma((2, 2)), dma((2,)), dma((6, 2)), dma((32, 2)),
            dma((8, 2)), dma((8,)), dma((6,)), dma((6,)),
            dma((12, 4)), dma((12,)), dma, dma((32, 4)), dma((32,)),
            dma((8,)), dma((8,)), dma((4,)),
        ],
        compiler_params=pltpu.CompilerParams(
            collective_id=1, has_side_effects=True, vmem_limit_bytes=52 << 20
        ),
        name="exchange",
    )(pan, child_blocks, child_rows, child_cols, child_rows, child_cols, child_count)


def finish(mode, front_ref, recv_ref, lrh_ref, lrl_ref, lch_ref, lcl_ref, corner_ref, out_ref, add_ref, code_ref):
    i=pl.program_id(0)
    r=lax.axis_index("row") if "nomesh" not in mode else 3
    c=lax.axis_index("col") if "nomesh" not in mode else 3
    @pl.when(i==0)
    def _():
        for s in range(16):
            code_ref[s]=jnp.max(recv_ref[s,258:259,:]).astype(jnp.int32)
    add_ref[...]=jnp.zeros_like(add_ref)
    if "noch" not in mode:
        def slot(s,carry):
            code=code_ref[s]
            @pl.when((code>>3)==i)
            def _():
                rows=recv_ref[s,256:257,:].astype(jnp.int32)
                cols=recv_ref[s,257:258,:].astype(jnp.int32)
                t=lax.broadcasted_iota(jnp.int32,(256,256),0)
                R=jnp.where(rows==t,1.0,0.0).astype(BF)
                Q=jnp.where(cols==t,1.0,0.0).astype(BF)
                h,l=split(recv_ref[s,0:256,:])
                p=bdot(R,h,NN)+bdot(R,l,NN)
                h,l=split(p)
                j=code&7
                add_ref[j]=add_ref[j]+(bdot(h,Q,NT)+bdot(l,Q,NT))
            return carry
        lax.fori_loop(0,16,slot,0)
    special=jnp.logical_and(i==0,r<2)
    ah=lrh_ref[0]; al=lrl_ref[0]
    for j in range(8):
        bh=lch_ref[j]; bl=lcl_ref[j]
        if "noup" in mode: u=0.0
        else: u=bdot(ah,bh,NT)+(bdot(ah,bl,NT)+bdot(al,bh,NT))
        v=front_ref[0,:,j,:]+add_ref[j]-u
        out_ref[0,:,j,:]=v
    @pl.when(c<2)
    def _():
        @pl.when(c==0)
        def _(): out_ref[0,:,0,:]=ah[:,0:256].astype(F32)+al[:,0:256].astype(F32)
        @pl.when(c==1)
        def _(): out_ref[0,:,0,:]=ah[:,256:512].astype(F32)+al[:,256:512].astype(F32)
    @pl.when(special)
    def _():
        out_ref[0,:,1:8,:]=jnp.zeros((256,7,256),F32)
        out_ref[0,:,0,:]=corner_ref[...]
def kernel_b(mode,front,recv,lrh,lrl,lch,lcl,corner):
    return pl.pallas_call(functools.partial(finish,mode),grid=(4,),
        out_shape=jax.ShapeDtypeStruct((4,256,8,256),F32),
        in_specs=[pl.BlockSpec((1,256,8,256),lambda i:(i,0,0,0)),
                  pl.BlockSpec((16,264,256),lambda i:(0,0,0)),
                  pl.BlockSpec((1,256,512),lambda i:(i,0,0)),pl.BlockSpec((1,256,512),lambda i:(i,0,0)),
                  pl.BlockSpec((8,256,512),lambda i:(0,0,0)),pl.BlockSpec((8,256,512),lambda i:(0,0,0)),
                  pl.BlockSpec((256,256),lambda i:(0,0))],
        out_specs=pl.BlockSpec((1,256,8,256),lambda i:(i,0,0,0)),
        scratch_shapes=[pltpu.VMEM((8,256,256),F32),pltpu.SMEM((16,),jnp.int32)],
        compiler_params=pltpu.CompilerParams(vmem_limit_bytes=48<<20),name="finish_"+mode.replace(" ","_"))(front,recv,lrh,lrl,lch,lcl,corner)


def local(front, child_blocks, child_rows, child_cols, child_count):
    pan = front[:, :, 0, :]
    recv, lrh, lrl, lch, lcl, corner = exchange(pan, child_blocks, child_rows, child_cols, child_count)
    return kernel_b("", front, recv, lrh, lrl, lch, lcl, corner)


def solution(mesh):
    placed = (
        P(None, "row", None, "col"),
        P(("row", "col"), None, None),
        P(("row", "col"), None),
        P(("row", "col"), None),
        P(("row", "col")),
    )
    return jax.shard_map(
        local, mesh=mesh, in_specs=placed, out_specs=P(None, "row", None, "col"), check_vma=False
    )
```

time: 926 us -> 432 us (0.47)
  waiting for transfers between devices: 556 us -> 0 us
  Pallas kernels: 0 us -> 422 us
  other arithmetic: 119 us -> 0 us
  matrix products: 85.1 us -> 0 us
  loops' own time: 60.1 us -> 0 us
  local copies, waits for them, and re-layouts: 64.7 us -> 9.16 us
  between operations: 17.3 us -> 0.68 us
  starting transfers between devices: 15.8 us -> 0 us
    pallas_call x0 -> x2, Pallas kernels: none -> 422 us  [the longest x1 400 us: exchange(): pl.pallas_call(comm_kernel, out_shape=(jax.ShapeDtypeStruct((16, 264, 256...]
    psum x4 -> x0, waiting for transfers between devices: 282 us -> none  [spread(): return lax.psum(block, axis)]
    all_gather x2 -> x0, waiting for transfers between devices: 234 us -> none  [local(): gathered = lax.all_gather(row_factor[:, None], 'row', axis=1, tiled=True)]
    another operation x21 -> x0, other arithmetic: 108 us -> none  [the longest x13 68.7 us: local(): diag_factor = jnp.linalg.cholesky((pivot_block + pivot_block.T) * 0.5)]
    dot_general x34 -> x0, matrix products: 79.6 us -> none  [the longest x16 32.3 us: add_slot(): placed = jnp.dot(placed, col_map, precision=lax.Precision.HIGHEST)]
    another operation x3 -> x0, loops' own time: 60.1 us -> none  [the longest x1 59.6 us: local(): front_work = lax.fori_loop(0, slot_count, add_slot, front)]
    all_to_all x3 -> x0, waiting for transfers between devices: 40.3 us -> none  [the longest x1 38.1 us: local(): lax.all_to_all(packed.reshape(col_count, CAP, block_size, block_size), 'c...]
    dynamic_slice x48 -> x0, local copies, waits for them, and re-layouts: 19.2 us -> none  [the longest x32 19 us: add_slot(): start = (local_row[slot], zero, local_col[slot], zero)]
  transfers between devices with their start and end apart: 9 -> 0, of which waited for: 8 -> 0; matrix products, arithmetic and copies ran while one was open for 2% -> 0% of each run, Pallas kernels for 0% -> 0%
where the time goes in v1:
time: 432 us; the launch traced here: 431 us
  Pallas kernels  422 us (98%)
  local copies, waits for them, and re-layouts  9.16 us (2%)
    pallas_call x1, Pallas kernels, exchange(): pl.pallas_call(comm_kernel, out_shape=(jax.ShapeDtypeStruct((16, 264, 256...  400 us
    pallas_call x1, Pallas kernels, kernel_b(): pl.pallas_call(functools.partial(finish, mode), grid=(4,), out_shape=jax....  21.2 us

profile of v1, /device:TPU:11, one launch (start us, length us, event | category | flops | bytes accessed | tf_op | source)
XLA Modules:
  0.0 431.5 jit_solution(9752650501353746292)
XLA Ops:
  0.7 3.9 slice.3
  4.6 1.0 copy.9
  5.6 0.0 copy-start.2
  5.6 0.7 copy-done.2
  6.3 0.0 copy-start.3
  6.3 0.7 copy-done.3
  7.0 400.5 %exchange.1 = (f32[16,264,256]{2,1,0:T(8,128)}, bf16[4,256,512]{2,1,0:T(8,128)(2,1)S(1)}, bf16[4,256,512]{2,1,0:T(8,128)(2,1)}, bf16[8,256,512]{2,1,0:T(8,128)(2...) custom-call(f32[4,256,256]{2,1,0:T(8,128)} %bitcast.3, f32[8,256,256]{2,1,0:T(8,128)} %cb.1, ...), custom_call_target="tpu_custom_call" | custom-call | tf_op jit(solution)/shard_map/exchange/pallas_call | solution.py:525
  407.5 0.0 copy-start
  407.5 1.6 copy-done
  409.1 0.0 copy-start.1
  409.1 1.2 copy-done.1
  410.3 21.2 %finish_.1 = f32[4,256,8,256]{3,2,1,0:T(8,128)} custom-call(f32[4,256,8,256]{3,2,1,0:T(8,128)} %front_ref.1, f32[16,264,256]{2,1,0:T(8,128)} %get-tuple-element.11.recv_ref, bf16[4,256,512]{2,1,0:T(8,128)(2,1)S(1)} %get-tuple-element.12.lrh_ref, bf16[4,256,512]{2,1,0:T(8,128)(2,1)S(1)} %copy-done.1, bf16[8,256,512]{2,1,0:T(8,128)(2,1)S(1)} %copy-done, ...), custom_call_target="tpu_custom_call" | custom-call | tf_op jit(solution)/shard_map/finish_/pallas_call | solution.py:604
Async XLA Ops:
  5.6 0.7 copy-start.2
  6.3 0.7 copy-start.3
  407.5 1.6 copy-start
  409.1 1.2 copy-start.1

commit v2 on v1

--- a/solution.py
+++ b/solution.py
@@ -87,6 +87,10 @@
     lax.fori_loop(0,4,tile,0)
 
 
+YH = 2
+NH = 1
+
+
 def m4(v):
     return lax.rem(v + 8, 4)
 
@@ -201,14 +205,15 @@
         p, br = lax.rem(j, 2), 1 + j // 2
         return rcopy(PR.at[p, br], PR.at[p, br], h4.at[j, 0], h4.at[j, 1], other)
 
-    def xz_index(q):
-        i, s = q // 4, lax.rem(q, 4)
-        return lax.rem(s, 2), s // 2, lax.rem(i, 2), lax.rem(i // 2 + 1, 4)
-
-    def h5_copy(q):
-        kk, src, p, br = xz_index(q)
-        ref = PC.at[kk, src, p, br]
-        return rcopy(ref, ref, h5.at[q, 0], h5.at[q, 1], other)
+    def xz_index(i, s):
+        ii = i // NH
+        rows = pl.ds(lax.rem(i, NH) * (256 // NH), 256 // NH)
+        return lax.rem(s, 2), s // 2, lax.rem(ii, 2), lax.rem(ii // 2 + 1, 4), rows
+
+    def h5_copy(i, src):
+        kk, src, p, br, rows = xz_index(i, 2 * src)
+        ref = PC.at[kk, src, p, br, rows]
+        return rcopy(ref, ref, h5.at[2 * i + src, 0], h5.at[2 * i + src, 1], other)
 
     def y0_parts(j):
         p, qt = j // 4, lax.rem(j, 4)
@@ -256,6 +261,16 @@
             def _():
                 back.start()
 
+            p = j // 4
+
+            @pl.when(jnp.logical_or(r == 1, jnp.logical_and(r == 0, p == 0)))
+            def _():
+                dj = j + 4 * jnp.minimum(r, 1)
+                (is_src, conds, copies), d, rows = d_parts(dj)
+                DG[d, rows, :] = PR[p, 0, rows, :]
+                for cp in copies:
+                    cp.start()
+
             return carry
 
         lax.fori_loop(0, 8, y0_step, 0)
@@ -265,18 +280,13 @@
         def d_step(j, carry):
             (is_src, conds, copies), d, rows = d_parts(j)
 
-            @pl.when(is_src)
-            def _():
-                DG[d, rows, :] = PR[d // 2, 0, rows, :]
-
             @pl.when(jnp.logical_not(is_src))
             def _():
                 copies[0].wait_recv()
-
-            for cond, cp in zip(conds, copies):
-                @pl.when(cond)
-                def _(cp=cp):
-                    cp.start()
+                for cond, cp in zip(conds, copies):
+                    @pl.when(cond)
+                    def _(cp=cp):
+                        cp.start()
 
             return carry
 
@@ -298,33 +308,40 @@
         lax.fori_loop(0, 6, h4_wait, 0)
 
         def h5_wait(q, carry):
-            @pl.when(lax.rem(q, 2) == 0)
-            def _():
-                h5_copy(q).wait_recv()
-
-            return carry
-
-        lax.fori_loop(0, 32, h5_wait, 0)
-
-    def y1_parts(j):
-        p, br = lax.rem(j, 2), 1 + j // 2
+            h5_copy(q // 2, lax.rem(q, 2)).wait_recv()
+            return carry
+
+        lax.fori_loop(0, 16 * NH, h5_wait, 0)
+
+    def y1_parts(i, p):
+        br = 1 + i // YH
+        rows = pl.ds(lax.rem(i, YH) * (256 // YH), 256 // YH)
         s = 1 - 2 * p
         yy = m4(s * y)
-        ref = PR.at[p, br]
-        return yy, rcopy(ref, ref, y1s.at[j], y1r.at[j], dev(z, x, m4(y + s), k))
-
-    def xz_parts(q):
-        kk, src, p, br = xz_index(q)
-        i = q // 4
-        row = 2 * y + kk + 8 * src
-        ref = PC.at[kk, src, p, br]
+        ref = PR.at[p, br, rows]
+        j = 2 * i + p
+        return yy, br, rcopy(ref, ref, y1s.at[j], y1r.at[j], dev(z, x, m4(y + s), k))
+
+    def xz_place(s):
+        row = 2 * y + lax.rem(s, 2) + 8 * (s // 2)
+        return row // 4, lax.rem(row, 4)
+
+    def xz_parts(i, s):
+        kk, src, p, br, rows = xz_index(i, s)
+        ref = PC.at[kk, src, p, br, rows]
         xfirst = lax.rem(i, 2)
         s1 = 1 - 2 * lax.rem(i // 2, 2)
         s2 = 1 - 2 * lax.rem(i // 4, 2)
+        q = 4 * i + s
+        sz, sx = xz_place(s)
         return tree(
-            row // 4, lax.rem(row, 4), xfirst, s1, s2,
-            lambda e, to: rcopy(ref, ref, xs_.at[q, e], xr_.at[q], to),
+            sz, sx, xfirst, s1, s2, lambda e, to: rcopy(ref, ref, xs_.at[q, e], xr_.at[q], to)
         )
+
+    def depth(s):
+        sz, sx = xz_place(s)
+        oz, ox = m4(z - sz), m4(x - sx)
+        return jnp.minimum(oz, 4 - oz) + jnp.minimum(ox, 4 - ox)
 
     @pl.when(k == 1)
     def _():
@@ -334,50 +351,73 @@
             h1_copy.start()
             h0_copy.wait_recv()
 
-        def y1_step(j, carry):
-            yy, fwd = y1_parts(j)
-
-            @pl.when(yy != 0)
-            def _():
-                fwd.wait_recv()
-
-            @pl.when(yy < 3)
-            def _():
-                fwd.start()
-
-            h4_copy(j).start()
-            return carry
-
-        lax.fori_loop(0, 6, y1_step, 0)
+        def xz_source(p, br):
+            @pl.when(lax.rem(r, 8) // 2 == y)
+            def _():
+                kk, src = lax.rem(r, 2), r // 8
+                PC[kk, src, p, br] = PR[p, br]
+                for h in range(NH):
+                    i = (p + 2 * lax.rem(br + 3, 4)) * NH + h
+                    is_src, conds, copies = xz_parts(i, src * 2 + kk)
+                    for cp in copies:
+                        cp.start()
+
+                    @pl.when(kk == 0)
+                    def _(i=i):
+                        h5_copy(i, src).start()
+
+        def y1_step(q, carry):
+            p = lax.rem(q, 2)
+            yy = m4((1 - 2 * p) * y)
+            i = q // 2 - jnp.maximum(yy - 1, 0)
+
+            @pl.when(jnp.logical_and(i >= 0, i < 3 * YH))
+            def _():
+                _, br, fwd = y1_parts(i, p)
+
+                @pl.when(yy != 0)
+                def _():
+                    fwd.wait_recv()
+
+                @pl.when(yy < 3)
+                def _():
+                    fwd.start()
+
+                @pl.when(lax.rem(i, YH) == YH - 1)
+                def _():
+                    h4_copy(p + 2 * (br - 1)).start()
+                    xz_source(p, br)
+
+            return carry
+
+        lax.fori_loop(0, 2 * (3 * YH + 2), y1_step, 0)
+        for p in range(2):
+            h2_copy[p].wait_recv()
+            xz_source(p, 0)
         pack()
         start_children()
-        for p in range(2):
-            h2_copy[p].wait_recv()
 
         def xz_step(q, carry):
-            is_src, conds, copies = xz_parts(q)
-            kk, src, p, br = xz_index(q)
-
-            @pl.when(is_src)
-            def _():
-                PC[kk, src, p, br] = PR[p, br]
-
-            @pl.when(jnp.logical_not(is_src))
-            def _():
+            s = lax.rem(q, 4)
+            dep = depth(s)
+            i = q // 4 - (dep - 1)
+
+            @pl.when(jnp.logical_and(dep > 0, jnp.logical_and(i >= 0, i < 8 * NH)))
+            def _():
+                is_src, conds, copies = xz_parts(i, s)
                 copies[0].wait_recv()
-
-            for cond, cp in zip(conds, copies):
-                @pl.when(cond)
-                def _(cp=cp):
-                    cp.start()
-
-            @pl.when(kk == 0)
-            def _():
-                h5_copy(q).start()
-
-            return carry
-
-        lax.fori_loop(0, 32, xz_step, 0)
+                for cond, cp in zip(conds, copies):
+                    @pl.when(cond)
+                    def _(cp=cp):
+                        cp.start()
+
+                @pl.when(lax.rem(s, 2) == 0)
+                def _():
+                    h5_copy(i, s // 2).start()
+
+            return carry
+
+        lax.fori_loop(0, 4 * (8 * NH + 3), xz_step, 0)
         h3_copy.wait_recv()
 
     i0 = lax.broadcasted_iota(jnp.int32, (256, 256), 0)
@@ -485,32 +525,39 @@
         def _():
             h1_copy.wait_send()
 
-        def y1_end(j, carry):
-            yy, fwd = y1_parts(j)
+        def y1_end(q, carry):
+            yy, br, fwd = y1_parts(q // 2, lax.rem(q, 2))
 
             @pl.when(yy < 3)
             def _():
                 fwd.wait_send()
 
+            return carry
+
+        lax.fori_loop(0, 6 * YH, y1_end, 0)
+
+        def h4_end(j, carry):
             h4_copy(j).wait_send()
             return carry
 
-        lax.fori_loop(0, 6, y1_end, 0)
+        lax.fori_loop(0, 6, h4_end, 0)
 
         def xz_end(q, carry):
-            is_src, conds, copies = xz_parts(q)
+            is_src, conds, copies = xz_parts(q // 4, lax.rem(q, 4))
             for cond, cp in zip(conds, copies):
                 @pl.when(cond)
                 def _(cp=cp):
                     cp.wait_send()
 
-            @pl.when(lax.rem(q, 2) == 0)
-            def _():
-                h5_copy(q).wait_send()
-
-            return carry
-
-        lax.fori_loop(0, 32, xz_end, 0)
+            return carry
+
+        lax.fori_loop(0, 32 * NH, xz_end, 0)
+
+        def h5_end(q, carry):
+            h5_copy(q // 2, lax.rem(q, 2)).wait_send()
+            return carry
+
+        lax.fori_loop(0, 16 * NH, h5_end, 0)
 
     wait_children()
     for cp in outs:
@@ -544,9 +591,9 @@
             pltpu.VMEM((3, 256, 256), BF),
             pltpu.VMEM((12, 256, 512), BF),
             pltpu.VMEM((12, 256, 512), BF),
-            dma((2,)), dma((2,)), dma((2, 2)), dma((2,)), dma((6, 2)), dma((32, 2)),
-            dma((8, 2)), dma((8,)), dma((6,)), dma((6,)),
-            dma((12, 4)), dma((12,)), dma, dma((32, 4)), dma((32,)),
+            dma((2,)), dma((2,)), dma((2, 2)), dma((2,)), dma((6, 2)), dma((16 * NH, 2)),
+            dma((8, 2)), dma((8,)), dma((6 * YH,)), dma((6 * YH,)),
+            dma((12, 4)), dma((12,)), dma, dma((32 * NH, 4)), dma((32 * NH,)),
             dma((8,)), dma((8,)), dma((4,)),
         ],
         compiler_params=pltpu.CompilerParams(

time: 432 us -> 135 us (0.31)
  Pallas kernels: 422 us -> 124 us
    pallas_call x1, Pallas kernels: 400 us -> 104 us  [exchange(): pl.pallas_call(comm_kernel, out_shape=(jax.ShapeDtypeStruct((16, 264, 256...]
where the time goes in v2:
time: 135 us; the launch traced here: 134 us
  Pallas kernels  124 us (92%)
  local copies, waits for them, and re-layouts  9.16 us (7%)
    pallas_call x1, Pallas kernels, exchange(): pl.pallas_call(comm_kernel, out_shape=(jax.ShapeDtypeStruct((16, 264, 256...  104 us
    pallas_call x1, Pallas kernels, kernel_b(): pl.pallas_call(functools.partial(finish, mode), grid=(4,), out_shape=jax....  19.8 us
    unnamed x9, local copies, waits for them, and re-layouts  5.24 us
    slice x1, local copies, waits for them, and re-layouts, local(): pan = front[:, :, 0, :]  3.92 us

profile of v2, /device:TPU:11, one launch (start us, length us, event | category | flops | bytes accessed | tf_op | source)
XLA Modules:
  0.0 133.8 jit_solution(10585316236012199254)
XLA Ops:
  0.7 3.9 %slice.3 = f32[4,256,1,256]{3,2,1,0:T(1,128)S(1)} slice(f32[4,256,8,256]{3,2,1,0:T(8,128)} %front_ref.1), slice={[0:4], [0:256], [0:1], [0:256]} | slice | bytes 2097152 | tf_op jit(solution)/shard_map/slice | solution.py:664
  4.6 1.0 copy.9
  5.6 0.0 copy-start.2
  5.6 0.7 copy-done.2
  6.3 0.0 copy-start.3
  6.3 0.7 copy-done.3
  7.0 104.2 %exchange.1 = (f32[16,264,256]{2,1,0:T(8,128)}, bf16[4,256,512]{2,1,0:T(8,128)(2,1)S(1)}, bf16[4,256,512]{2,1,0:T(8,128)(2,1)}, bf16[8,256,512]{2,1,0:T(8,128)(2...) custom-call(f32[4,256,256]{2,1,0:T(8,128)} %bitcast.3, f32[8,256,256]{2,1,0:T(8,128)} %cb.1, ...), custom_call_target="tpu_custom_call" | custom-call | tf_op jit(solution)/shard_map/exchange/pallas_call | solution.py:572
  111.2 0.0 copy-start
  111.2 1.6 %copy-done = bf16[8,256,512]{2,1,0:T(8,128)(2,1)S(1)} copy-done((bf16[8,256,512]{2,1,0:T(8,128)(2,1)S(1)}, bf16[8,256,512]{2,1,0:T(8,128)(2,1)}, u32[]{:S(2)}) %copy-start) | copy-done | bytes 2097176
  112.8 0.0 copy-start.1
  112.8 1.2 copy-done.1
  114.0 19.8 %finish_.1 = f32[4,256,8,256]{3,2,1,0:T(8,128)} custom-call(f32[4,256,8,256]{3,2,1,0:T(8,128)} %front_ref.1, f32[16,264,256]{2,1,0:T(8,128)} %get-tuple-element.11.recv_ref, bf16[4,256,512]{2,1,0:T(8,128)(2,1)S(1)} %get-tuple-element.12.lrh_ref, bf16[4,256,512]{2,1,0:T(8,128)(2,1)S(1)} %copy-done.1, bf16[8,256,512]{2,1,0:T(8,128)(2,1)S(1)} %copy-done, ...), custom_call_target="tpu_custom_call" | custom-call | tf_op jit(solution)/shard_map/finish_/pallas_call | solution.py:651
Async XLA Ops:
  5.6 0.7 copy-start.2
  6.3 0.7 copy-start.3
  111.2 1.6 %copy-start = (bf16[8,256,512]{2,1,0:T(8,128)(2,1)S(1)}, bf16[8,256,512]{2,1,0:T(8,128)(2,1)}, u32[]{:S(2)}) copy-start(bf16[8,256,512]{2,1,0:T(8,128)(2,1)} %get-tuple-element.14.lch_ref) | copy-start | bytes 6291460
  112.8 1.2 copy-start.1

commit v3 on v1

--- a/solution.py
+++ b/solution.py
@@ -87,6 +87,13 @@
     lax.fori_loop(0,4,tile,0)
 
 
+DQ = 2
+YH = 4
+CSTEP = 4
+LAG = 1
+NH = 1
+
+
 def m4(v):
     return lax.rem(v + 8, 4)
 
@@ -95,12 +102,15 @@
     pan, cb, crow, ccol, crow_s, ccol_s, cnt_s,
     recv, lrh, lrl, lch, lcl, corner,
     stage, PR, PC, DG, AW, Wh, Wl, oh, ol,
-    h0, h1, h2, h3, h4, h5, y0s, y0r, y1s, y1r, ds, dr, dloc, xs_, xr_, cs, cr, osem,
+    h1, h3, h4, h5, y0s, y0r, y1s, y1r, ds, dr, dloc, xs_, xr_, cs, cr, osem,
 ):
     r = lax.axis_index("row")
     c = lax.axis_index("col")
     z, x = r // 4, lax.rem(r, 4)
     y, k = c // 2, lax.rem(c, 2)
+    zp, zm = jnp.where(z == 3, 0, z + 1), jnp.where(z == 0, 3, z - 1)
+    xp, xm = jnp.where(x == 3, 0, x + 1), jnp.where(x == 0, 3, x - 1)
+    yp, ym = jnp.where(y == 3, 0, y + 1), jnp.where(y == 0, 3, y - 1)
 
     def dev(z, x, y, k):
         return (z * 4 + x, y * 2 + k)
@@ -168,86 +178,105 @@
         for d in range(1, 8):
             child_copy(d).wait()
 
-    def tree(src_z, src_x, xfirst, s1, s2, make):
-        oz, ox = z - src_z, x - src_x
-        a = m4(s1 * jnp.where(xfirst == 1, ox, oz))
-        bb = m4(s2 * jnp.where(xfirst == 1, oz, ox))
-        dz1, dx1 = jnp.where(xfirst == 1, 0, s1), jnp.where(xfirst == 1, s1, 0)
-        dz2, dx2 = jnp.where(xfirst == 1, s2, 0), jnp.where(xfirst == 1, 0, s2)
-        is_src = jnp.logical_and(a == 0, bb == 0)
+    def both(v):
+        f = lax.rem(v + 4, 4)
+        return f, jnp.where(f == 0, 0, 4 - f)
+
+    def tree(oz, ox, xfirst, back1, back2, make):
+        def pick(flag, a, b):
+            if isinstance(flag, bool):
+                return a if flag else b
+            return jnp.where(flag, a, b)
+
+        a = pick(xfirst, pick(back1, ox[1], ox[0]), pick(back1, oz[1], oz[0]))
+        bb = pick(xfirst, pick(back2, oz[1], oz[0]), pick(back2, ox[1], ox[0]))
+        row = z * 4 + x
+        z_up, z_dn, x_up, x_dn = zp * 4 + x, zm * 4 + x, z * 4 + xp, z * 4 + xm
+        up1, dn1 = pick(xfirst, x_up, z_up), pick(xfirst, x_dn, z_dn)
+        up2, dn2 = pick(xfirst, z_up, x_up), pick(xfirst, z_dn, x_dn)
+        is_src = a + bb == 0
         conds = (
             jnp.logical_and(bb == 0, a <= 1),
-            jnp.logical_and(bb == 0, a == 0),
+            is_src,
             bb <= 1,
             bb == 0,
         )
         targets = (
-            dev(m4(z + dz1), m4(x + dx1), y, k),
-            dev(m4(z - dz1), m4(x - dx1), y, k),
-            dev(m4(z + dz2), m4(x + dx2), y, k),
-            dev(m4(z - dz2), m4(x - dx2), y, k),
+            (pick(back1, dn1, up1), c), (pick(back1, up1, dn1), c),
+            (pick(back2, dn2, up2), c), (pick(back2, up2, dn2), c),
         )
         copies = [make(e, to) for e, to in enumerate(targets)]
         return is_src, conds, copies
 
-    h0_copy = rcopy(pan.at[pl.ds(1, 3)], PR.at[0, pl.ds(1, 3)], h0.at[0], h0.at[1], other)
-    h1_copy = rcopy(pan.at[0], PR.at[1, 0], h1.at[0], h1.at[1], other)
-    h2_copy = [
-        rcopy(PR.at[p, 0], PR.at[p, 0], h2.at[p, 0], h2.at[p, 1], other) for p in range(2)
+    h1_copies = [
+        rcopy(pan.at[i], PR.at[2 * i + 1], h1.at[i, 0], h1.at[i, 1], other) for i in range(4)
     ]
     h3_copy = rcopy(AW, AW, h3.at[0], h3.at[1], other)
 
     def h4_copy(j):
-        p, br = lax.rem(j, 2), 1 + j // 2
-        return rcopy(PR.at[p, br], PR.at[p, br], h4.at[j, 0], h4.at[j, 1], other)
-
-    def xz_index(q):
-        i, s = q // 4, lax.rem(q, 4)
-        return lax.rem(s, 2), s // 2, lax.rem(i, 2), lax.rem(i // 2 + 1, 4)
-
-    def h5_copy(q):
-        kk, src, p, br = xz_index(q)
-        ref = PC.at[kk, src, p, br]
-        return rcopy(ref, ref, h5.at[q, 0], h5.at[q, 1], other)
+        return rcopy(PR.at[j], PR.at[j], h4.at[j, 0], h4.at[j, 1], other)
+
+    y_depth = (y, jnp.where(y == 0, 0, 4 - y))
+    y_next = (dev(z, x, yp, k), dev(z, x, ym, k))
+
+    def y1_part(br, p, h):
+        rows = pl.ds(h * (256 // YH), 256 // YH)
+        ref = PR.at[2 * br + p, rows]
+        j = (2 * br + p) * YH + h
+        return rcopy(ref, ref, y1s.at[j], y1r.at[j], y_next[p])
+
+    def h5_copy(i, src, h):
+        ref = PC.at[2 * src, i, pl.ds(h * (256 // NH), 256 // NH)]
+        j = (2 * i + src) * NH + h
+        return rcopy(ref, ref, h5.at[j, 0], h5.at[j, 1], other)
 
     def y0_parts(j):
-        p, qt = j // 4, lax.rem(j, 4)
-        s = 1 - 2 * p
-        yy = m4(s * y)
-        ref = PR.at[p, 0, pl.ds(qt * 64, 64)]
-        fwd = rcopy(ref, ref, y0s.at[j, 0], y0r.at[j], dev(z, x, m4(y + s), k))
-        back = rcopy(ref, ref, y0s.at[j, 1], y0r.at[j], dev(z, x, m4(y - s), k))
-        return yy, fwd, back
+        p, qt = j // DQ, j % DQ
+        ref = PR.at[p, pl.ds(qt * (256 // DQ), 256 // DQ)]
+        fwd = rcopy(ref, ref, y0s.at[j, 0], y0r.at[j], y_next[p])
+        back = rcopy(ref, ref, y0s.at[j, 1], y0r.at[j], y_next[1 - p])
+        return p, y_depth[p], fwd, back
+
+    dz_ = both(z)
+    dx_ = (both(x), both(x - 1))
 
     def d_parts(j):
-        d, qt = j // 4, lax.rem(j, 4)
-        rows = pl.ds(qt * 64, 64)
+        d, qt = j // DQ, j % DQ
+        rows = pl.ds(qt * (256 // DQ), 256 // DQ)
         ref = DG.at[d, rows]
-        src_x = jnp.minimum(d, 1)
-        s1 = 1 - 2 * lax.rem(d, 2)
+        back = d % 2 == 1
         parts = tree(
-            0, src_x, 1, s1, s1, lambda e, to: rcopy(ref, ref, ds.at[j, e], dr.at[j], to)
+            dz_, dx_[min(d, 1)], True, back, back,
+            lambda e, to: rcopy(ref, ref, ds.at[j, e], dr.at[j], to),
         )
         return parts, d, rows
 
+    def d_sources(p, qt):
+        for row in (0, 1) if p == 0 else (1,):
+            @pl.when(r == row)
+            def _(row=row):
+                d = row + p
+                (is_src, conds, copies), d, rows = d_parts(d * DQ + qt)
+                DG[d, rows, :] = PR[p, rows, :]
+                for cp in copies:
+                    cp.start()
+
     @pl.when(k == 0)
     def _():
         @pl.when(y == 0)
         def _():
-            h0_copy.start()
-            PR[0, 0] = pan[0]
-
-        def y0_step(j, carry):
-            yy, fwd, back = y0_parts(j)
+            for i in range(4):
+                PR[2 * i] = pan[i]
+            for cp in h1_copies:
+                cp.wait_recv()
+
+        for j in range(2 * DQ):
+            p, yy, fwd, back = y0_parts(j)
 
             @pl.when(yy != 0)
             def _():
                 fwd.wait_recv()
 
-            @pl.when(jnp.logical_and(yy == 0, j == 4))
-            def _():
-                h1_copy.wait_recv()
-
             @pl.when(yy <= 1)
             def _():
                 fwd.start()
@@ -256,31 +285,46 @@
             def _():
                 back.start()
 
-            return carry
-
-        lax.fori_loop(0, 8, y0_step, 0)
-        for p in range(2):
-            h2_copy[p].start()
-
-        def d_step(j, carry):
+            if j % DQ == DQ - 1:
+                h4_copy(p).start()
+            d_sources(p, j % DQ)
+
+        def y1_step(t, carry):
+            for h in range(YH):
+                for p in range(2):
+                    yy = y_depth[p]
+                    br = t - yy
+
+                    @pl.when(jnp.logical_and(br >= 1, br <= 3))
+                    def _(p=p, yy=yy, br=br, h=h):
+                        fwd = y1_part(br, p, h)
+
+                        @pl.when(yy != 0)
+                        def _():
+                            fwd.wait_recv()
+
+                        @pl.when(yy < 3)
+                        def _():
+                            fwd.start()
+
+                        if h == YH - 1:
+                            h4_copy(2 * br + p).start()
+
+            return carry
+
+        lax.fori_loop(1, 7, y1_step, 0)
+
+        for j in range(3 * DQ):
             (is_src, conds, copies), d, rows = d_parts(j)
-
-            @pl.when(is_src)
-            def _():
-                DG[d, rows, :] = PR[d // 2, 0, rows, :]
 
             @pl.when(jnp.logical_not(is_src))
             def _():
                 copies[0].wait_recv()
-
-            for cond, cp in zip(conds, copies):
-                @pl.when(cond)
-                def _(cp=cp):
-                    cp.start()
-
-            return carry
-
-        lax.fori_loop(0, 12, d_step, 0)
+                for cond, cp in zip(conds, copies):
+                    @pl.when(cond)
+                    def _(cp=cp):
+                        cp.start()
+
         pack()
         start_children()
 
@@ -291,93 +335,85 @@
         factor(AW)
         h3_copy.start()
 
+        def h5_wait(i, carry):
+            for src in range(2):
+                for h in range(NH):
+                    h5_copy(i, src, h).wait_recv()
+            return carry
+
+        lax.fori_loop(0, 8, h5_wait, 0)
+
+    xz_off = []
+    xz_depth = []
+    for s in range(4):
+        row = 2 * y + s % 2 + 8 * (s // 2)
+        oz, ox = both(z - row // 4), both(x - lax.rem(row, 4))
+        xz_off.append((oz, ox))
+        xz_depth.append(jnp.minimum(oz[0], oz[1]) + jnp.minimum(ox[0], ox[1]))
+
+    def xz_parts(i, s, h):
+        ref = PC.at[s, i, pl.ds(h * (256 // NH), 256 // NH)]
+        zfirst = jnp.logical_or(i == 3, i == 7)
+        back1 = i >= 4
+        back2 = jnp.logical_or(jnp.logical_or(i == 1, i == 3), jnp.logical_or(i == 4, i == 6))
+        q = (4 * i + s) * NH + h
+        oz, ox = xz_off[s]
+        return tree(
+            oz, ox, jnp.logical_not(zfirst), back1, back2,
+            lambda e, to: rcopy(ref, ref, xs_.at[q, e], xr_.at[q], to),
+        )
+
+    @pl.when(k == 1)
+    def _():
+        @pl.when(y == 0)
+        def _():
+            for cp in h1_copies:
+                cp.start()
+
+        pack()
+
+        def xz_step(t, carry):
+            for h in range(NH):
+                for s in range(4):
+                    dep = xz_depth[s]
+                    i = t - LAG * dep
+
+                    @pl.when(jnp.logical_and(i >= 0, i < 8))
+                    def _(s=s, dep=dep, i=i, h=h):
+                        _, conds, copies = xz_parts(i, s, h)
+
+                        @pl.when(dep == 0)
+                        def _():
+                            if h == 0:
+                                h4_copy(i).wait_recv()
+                                PC[s, i] = PR[i]
+
+                        @pl.when(dep != 0)
+                        def _():
+                            copies[0].wait_recv()
+
+                        for cond, cp in zip(conds, copies):
+                            @pl.when(cond)
+                            def _(cp=cp):
+                                cp.start()
+
+                        if s % 2 == 0:
+                            h5_copy(i, s // 2, h).start()
+
+            return carry
+
+        lax.fori_loop(0, CSTEP, xz_step, 0)
+        start_children()
+        lax.fori_loop(CSTEP, 8 + 4 * LAG, xz_step, 0)
+
         def h4_wait(j, carry):
             h4_copy(j).wait_recv()
             return carry
 
-        lax.fori_loop(0, 6, h4_wait, 0)
-
-        def h5_wait(q, carry):
-            @pl.when(lax.rem(q, 2) == 0)
-            def _():
-                h5_copy(q).wait_recv()
-
-            return carry
-
-        lax.fori_loop(0, 32, h5_wait, 0)
-
-    def y1_parts(j):
-        p, br = lax.rem(j, 2), 1 + j // 2
-        s = 1 - 2 * p
-        yy = m4(s * y)
-        ref = PR.at[p, br]
-        return yy, rcopy(ref, ref, y1s.at[j], y1r.at[j], dev(z, x, m4(y + s), k))
-
-    def xz_parts(q):
-        kk, src, p, br = xz_index(q)
-        i = q // 4
-        row = 2 * y + kk + 8 * src
-        ref = PC.at[kk, src, p, br]
-        xfirst = lax.rem(i, 2)
-        s1 = 1 - 2 * lax.rem(i // 2, 2)
-        s2 = 1 - 2 * lax.rem(i // 4, 2)
-        return tree(
-            row // 4, lax.rem(row, 4), xfirst, s1, s2,
-            lambda e, to: rcopy(ref, ref, xs_.at[q, e], xr_.at[q], to),
-        )
-
-    @pl.when(k == 1)
-    def _():
-        @pl.when(y == 0)
+        @pl.when(lax.rem(r, 8) // 2 != y)
         def _():
-            PR[1, 1:4] = pan[1:4]
-            h1_copy.start()
-            h0_copy.wait_recv()
-
-        def y1_step(j, carry):
-            yy, fwd = y1_parts(j)
-
-            @pl.when(yy != 0)
-            def _():
-                fwd.wait_recv()
-
-            @pl.when(yy < 3)
-            def _():
-                fwd.start()
-
-            h4_copy(j).start()
-            return carry
-
-        lax.fori_loop(0, 6, y1_step, 0)
-        pack()
-        start_children()
-        for p in range(2):
-            h2_copy[p].wait_recv()
-
-        def xz_step(q, carry):
-            is_src, conds, copies = xz_parts(q)
-            kk, src, p, br = xz_index(q)
-
-            @pl.when(is_src)
-            def _():
-                PC[kk, src, p, br] = PR[p, br]
-
-            @pl.when(jnp.logical_not(is_src))
-            def _():
-                copies[0].wait_recv()
-
-            for cond, cp in zip(conds, copies):
-                @pl.when(cond)
-                def _(cp=cp):
-                    cp.start()
-
-            @pl.when(kk == 0)
-            def _():
-                h5_copy(q).start()
-
-            return carry
-
-        lax.fori_loop(0, 32, xz_step, 0)
+            lax.fori_loop(0, 8, h4_wait, 0)
+
         h3_copy.wait_recv()
 
     i0 = lax.broadcasted_iota(jnp.int32, (256, 256), 0)
@@ -403,7 +439,7 @@
             oh[i, :, pl.ds(p * 256, 256)] = hi
             ol[i, :, pl.ds(p * 256, 256)] = lo
 
-        solve(PR[0, i], PR[1, i], put)
+        solve(PR[2 * i], PR[2 * i + 1], put)
         return carry
 
     lax.fori_loop(0, 4, row_solve, 0)
@@ -413,7 +449,8 @@
             oh[4 + i, :, pl.ds(p * 256, 256)] = hi
             ol[4 + i, :, pl.ds(p * 256, 256)] = lo
 
-        solve(PC[k, lax.rem(i, 2), 0, i // 2], PC[k, lax.rem(i, 2), 1, i // 2], put)
+        row_set, j = k + 2 * lax.rem(i, 2), 2 * (i // 2)
+        solve(PC[row_set, j], PC[row_set, j + 1], put)
         return carry
 
     lax.fori_loop(0, 8, col_solve, 0)
@@ -446,12 +483,8 @@
 
     @pl.when(k == 0)
     def _():
-        @pl.when(y == 0)
-        def _():
-            h0_copy.wait_send()
-
-        def y0_end(j, carry):
-            yy, fwd, back = y0_parts(j)
+        for j in range(2 * DQ):
+            p, yy, fwd, back = y0_parts(j)
 
             @pl.when(yy <= 1)
             def _():
@@ -461,56 +494,54 @@
             def _():
                 back.wait_send()
 
-            return carry
-
-        lax.fori_loop(0, 8, y0_end, 0)
-        for p in range(2):
-            h2_copy[p].wait_send()
-
-        def d_end(j, carry):
+        def y1_end(br, carry):
+            for p in range(2):
+                @pl.when(y_depth[p] < 3)
+                def _(p=p):
+                    for h in range(YH):
+                        y1_part(br, p, h).wait_send()
+
+            return carry
+
+        lax.fori_loop(1, 4, y1_end, 0)
+
+        def h4_end(j, carry):
+            h4_copy(j).wait_send()
+            return carry
+
+        lax.fori_loop(0, 8, h4_end, 0)
+
+        for j in range(3 * DQ):
             (is_src, conds, copies), d, rows = d_parts(j)
             for cond, cp in zip(conds, copies):
                 @pl.when(cond)
                 def _(cp=cp):
                     cp.wait_send()
 
-            return carry
-
-        lax.fori_loop(0, 12, d_end, 0)
         h3_copy.wait_send()
 
     @pl.when(k == 1)
     def _():
         @pl.when(y == 0)
         def _():
-            h1_copy.wait_send()
-
-        def y1_end(j, carry):
-            yy, fwd = y1_parts(j)
-
-            @pl.when(yy < 3)
-            def _():
-                fwd.wait_send()
-
-            h4_copy(j).wait_send()
-            return carry
-
-        lax.fori_loop(0, 6, y1_end, 0)
-
-        def xz_end(q, carry):
-            is_src, conds, copies = xz_parts(q)
-            for cond, cp in zip(conds, copies):
-                @pl.when(cond)
-                def _(cp=cp):
-                    cp.wait_send()
-
-            @pl.when(lax.rem(q, 2) == 0)
-            def _():
-                h5_copy(q).wait_send()
-
-            return carry
-
-        lax.fori_loop(0, 32, xz_end, 0)
+            for cp in h1_copies:
+                cp.wait_send()
+
+        def xz_end(i, carry):
+            for s in range(4):
+                for h in range(NH):
+                    _, conds, copies = xz_parts(i, s, h)
+                    for cond, cp in zip(conds, copies):
+                        @pl.when(cond)
+                        def _(cp=cp):
+                            cp.wait_send()
+
+                    if s % 2 == 0:
+                        h5_copy(i, s // 2, h).wait_send()
+
+            return carry
+
+        lax.fori_loop(0, 8, xz_end, 0)
 
     wait_children()
     for cp in outs:
@@ -536,17 +567,17 @@
         out_specs=(hbm, hbm, hbm, hbm, hbm, vm),
         scratch_shapes=[
             pltpu.VMEM((16, 264, 256), F32),
-            pltpu.VMEM((2, 4, 256, 256), F32),
-            pltpu.VMEM((2, 2, 2, 4, 256, 256), F32),
+            pltpu.VMEM((8, 256, 256), F32),
+            pltpu.VMEM((4, 8, 256, 256), F32),
             pltpu.VMEM((3, 256, 256), F32),
             pltpu.VMEM((512, 512), F32),
             pltpu.VMEM((3, 256, 256), BF),
             pltpu.VMEM((3, 256, 256), BF),
             pltpu.VMEM((12, 256, 512), BF),
             pltpu.VMEM((12, 256, 512), BF),
-            dma((2,)), dma((2,)), dma((2, 2)), dma((2,)), dma((6, 2)), dma((32, 2)),
-            dma((8, 2)), dma((8,)), dma((6,)), dma((6,)),
-            dma((12, 4)), dma((12,)), dma, dma((32, 4)), dma((32,)),
+            dma((4, 2)), dma((2,)), dma((8, 2)), dma((16 * NH, 2)),
+            dma((8, 2)), dma((8,)), dma((8 * YH,)), dma((8 * YH,)),
+            dma((12, 4)), dma((12,)), dma, dma((32 * NH, 4)), dma((32 * NH,)),
             dma((8,)), dma((8,)), dma((4,)),
         ],
         compiler_params=pltpu.CompilerParams(

time: 432 us -> 127 us (0.29)
  Pallas kernels: 422 us -> 117 us
    pallas_call x1, Pallas kernels: 400 us -> 95.9 us  [exchange(): pl.pallas_call(comm_kernel, out_shape=(jax.ShapeDtypeStruct((16, 264, 256...]
where the time goes in v3:
time: 127 us
  Pallas kernels  117 us (92%)
  local copies, waits for them, and re-layouts  9.16 us (7%)
    pallas_call x1, Pallas kernels, exchange(): pl.pallas_call(comm_kernel, out_shape=(jax.ShapeDtypeStruct((16, 264, 256...  95.9 us
    pallas_call x1, Pallas kernels, kernel_b(): pl.pallas_call(functools.partial(finish, mode), grid=(4,), out_shape=jax....  21.2 us
    unnamed x9, local copies, waits for them, and re-layouts  5.24 us
    slice x1, local copies, waits for them, and re-layouts, local(): pan = front[:, :, 0, :]  3.92 us

profile of v3, /device:TPU:11, one launch (start us, length us, event | category | flops | bytes accessed | tf_op | source)
XLA Modules:
  0.0 127.0 jit_solution(4365016689634472007)
XLA Ops:
  0.7 3.9 %slice.3 = f32[4,256,1,256]{3,2,1,0:T(1,128)S(1)} slice(f32[4,256,8,256]{3,2,1,0:T(8,128)} %front_ref.1), slice={[0:4], [0:256], [0:1], [0:256]} | slice | bytes 2097152 | tf_op jit(solution)/shard_map/slice | solution.py:648
  4.6 1.0 copy.9
  5.6 0.0 copy-start.2
  5.6 0.7 copy-done.2
  6.3 0.0 copy-start.3
  6.3 0.7 copy-done.3
  7.0 95.9 %exchange.1 = (f32[16,264,256]{2,1,0:T(8,128)}, bf16[4,256,512]{2,1,0:T(8,128)(2,1)S(1)}, bf16[4,256,512]{2,1,0:T(8,128)(2,1)}, bf16[8,256,512]{2,1,0:T(8,128)(2...) custom-call(f32[4,256,256]{2,1,0:T(8,128)} %bitcast.3, f32[8,256,256]{2,1,0:T(8,128)} %cb.1, ...), custom_call_target="tpu_custom_call" | custom-call | tf_op jit(solution)/shard_map/exchange/pallas_call | solution.py:556
  103.0 0.0 copy-start
  103.0 1.6 %copy-done = bf16[8,256,512]{2,1,0:T(8,128)(2,1)S(1)} copy-done((bf16[8,256,512]{2,1,0:T(8,128)(2,1)S(1)}, bf16[8,256,512]{2,1,0:T(8,128)(2,1)}, u32[]{:S(2)}) %copy-start) | copy-done | bytes 2097176
  104.6 0.0 copy-start.1
  104.6 1.2 copy-done.1
  105.8 21.2 %finish_.1 = f32[4,256,8,256]{3,2,1,0:T(8,128)} custom-call(f32[4,256,8,256]{3,2,1,0:T(8,128)} %front_ref.1, f32[16,264,256]{2,1,0:T(8,128)} %get-tuple-element.11.recv_ref, bf16[4,256,512]{2,1,0:T(8,128)(2,1)S(1)} %get-tuple-element.12.lrh_ref, bf16[4,256,512]{2,1,0:T(8,128)(2,1)S(1)} %copy-done.1, bf16[8,256,512]{2,1,0:T(8,128)(2,1)S(1)} %copy-done, ...), custom_call_target="tpu_custom_call" | custom-call | tf_op jit(solution)/shard_map/finish_/pallas_call | solution.py:635
Async XLA Ops:
  5.6 0.7 copy-start.2
  6.3 0.7 copy-start.3
  103.0 1.6 %copy-start = (bf16[8,256,512]{2,1,0:T(8,128)(2,1)S(1)}, bf16[8,256,512]{2,1,0:T(8,128)(2,1)}, u32[]{:S(2)}) copy-start(bf16[8,256,512]{2,1,0:T(8,128)(2,1)} %get-tuple-element.14.lch_ref) | copy-start | bytes 6291460
  104.6 1.2 copy-start.1

commit v4 on v3

--- a/solution.py
+++ b/solution.py
@@ -99,10 +99,11 @@
 
 
 def comm_kernel(
-    pan, cb, crow, ccol, crow_s, ccol_s, cnt_s,
+    front, cb_in, crow, ccol, crow_s, ccol_s, cnt_s,
     recv, lrh, lrl, lch, lcl, corner,
-    stage, PR, PC, DG, AW, Wh, Wl, oh, ol,
-    h1, h3, h4, h5, y0s, y0r, y1s, y1r, ds, dr, dloc, xs_, xr_, cs, cr, osem,
+    fbuf, pan, cb, lsem,
+    stage, PR, PC, DG, AW, Wh, Wl,
+    h1, h3, h4, h5, y0s, y0r, y1s, y1r, ds, dr, dloc, xs_, xr_, cs, cr,
 ):
     r = lax.axis_index("row")
     c = lax.axis_index("col")
@@ -116,6 +117,18 @@
         return (z * 4 + x, y * 2 + k)
 
     other = dev(z, x, y, 1 - k)
+    front_copies = [
+        pltpu.make_async_copy(front.at[i], fbuf.at[i], lsem.at[i]) for i in range(4)
+    ]
+    cb_copy = pltpu.make_async_copy(cb_in, cb, lsem.at[4])
+
+    @pl.when(y == 0)
+    def _():
+        for cp in front_copies:
+            cp.start()
+
+    cb_copy.start()
+
     b = pltpu.get_barrier_semaphore()
     for d in range(1, 8):
         pl.semaphore_signal(b, inc=1, device_id=(r, lax.rem(c + d, 8)), device_id_type=MESH)
@@ -266,7 +279,8 @@
         @pl.when(y == 0)
         def _():
             for i in range(4):
-                PR[2 * i] = pan[i]
+                front_copies[i].wait()
+                PR[2 * i] = fbuf[i, :, 0, :]
             for cp in h1_copies:
                 cp.wait_recv()
 
@@ -325,6 +339,7 @@
                     def _(cp=cp):
                         cp.start()
 
+        cb_copy.wait()
         pack()
         start_children()
 
@@ -367,9 +382,12 @@
     def _():
         @pl.when(y == 0)
         def _():
-            for cp in h1_copies:
-                cp.start()
-
+            for i in range(4):
+                front_copies[i].wait()
+                pan[i] = fbuf[i, :, 0, :]
+                h1_copies[i].start()
+
+        cb_copy.wait()
         pack()
 
         def xz_step(t, carry):
@@ -436,8 +454,8 @@
 
     def row_solve(i, carry):
         def put(p, hi, lo):
-            oh[i, :, pl.ds(p * 256, 256)] = hi
-            ol[i, :, pl.ds(p * 256, 256)] = lo
+            lrh[i, :, pl.ds(p * 256, 256)] = hi
+            lrl[i, :, pl.ds(p * 256, 256)] = lo
 
         solve(PR[2 * i], PR[2 * i + 1], put)
         return carry
@@ -446,23 +464,14 @@
 
     def col_solve(i, carry):
         def put(p, hi, lo):
-            oh[4 + i, :, pl.ds(p * 256, 256)] = hi
-            ol[4 + i, :, pl.ds(p * 256, 256)] = lo
+            lch[i, :, pl.ds(p * 256, 256)] = hi
+            lcl[i, :, pl.ds(p * 256, 256)] = lo
 
         row_set, j = k + 2 * lax.rem(i, 2), 2 * (i // 2)
         solve(PC[row_set, j], PC[row_set, j + 1], put)
         return carry
 
     lax.fori_loop(0, 8, col_solve, 0)
-    outs = [
-        pltpu.make_async_copy(oh.at[pl.ds(0, 4)], lrh, osem.at[0]),
-        pltpu.make_async_copy(ol.at[pl.ds(0, 4)], lrl, osem.at[1]),
-        pltpu.make_async_copy(oh.at[pl.ds(4, 8)], lch, osem.at[2]),
-        pltpu.make_async_copy(ol.at[pl.ds(4, 8)], lcl, osem.at[3]),
-    ]
-    for cp in outs:
-        cp.start()
-
     corner[...] = jnp.zeros((256, 256), F32)
 
     def diag_block(o):
@@ -544,14 +553,12 @@
         lax.fori_loop(0, 8, xz_end, 0)
 
     wait_children()
-    for cp in outs:
-        cp.wait()
-
-
-def exchange(pan, child_blocks, child_rows, child_cols, child_count):
+
+
+def exchange(front, child_blocks, child_rows, child_cols, child_count):
     vm = pl.BlockSpec(memory_space=pltpu.VMEM)
     sm = pl.BlockSpec(memory_space=pltpu.SMEM)
-    hbm = pl.BlockSpec(memory_space=pl.ANY)
+    hbm = pl.BlockSpec(memory_space=pltpu.HBM)
     dma = pltpu.SemaphoreType.DMA
     return pl.pallas_call(
         comm_kernel,
@@ -563,9 +570,13 @@
             jax.ShapeDtypeStruct((8, 256, 512), BF),
             jax.ShapeDtypeStruct((256, 256), F32),
         ),
-        in_specs=[vm, vm, vm, vm, sm, sm, sm],
-        out_specs=(hbm, hbm, hbm, hbm, hbm, vm),
+        in_specs=[hbm, hbm, vm, vm, sm, sm, sm],
+        out_specs=(vm, vm, vm, vm, vm, vm),
         scratch_shapes=[
+            pltpu.VMEM((4, 256, 8, 256), F32),
+            pltpu.VMEM((4, 256, 256), F32),
+            pltpu.VMEM((8, 256, 256), F32),
+            dma((5,)),
             pltpu.VMEM((16, 264, 256), F32),
             pltpu.VMEM((8, 256, 256), F32),
             pltpu.VMEM((4, 8, 256, 256), F32),
@@ -573,18 +584,16 @@
             pltpu.VMEM((512, 512), F32),
             pltpu.VMEM((3, 256, 256), BF),
             pltpu.VMEM((3, 256, 256), BF),
-            pltpu.VMEM((12, 256, 512), BF),
-            pltpu.VMEM((12, 256, 512), BF),
             dma((4, 2)), dma((2,)), dma((8, 2)), dma((16 * NH, 2)),
             dma((8, 2)), dma((8,)), dma((8 * YH,)), dma((8 * YH,)),
             dma((12, 4)), dma((12,)), dma, dma((32 * NH, 4)), dma((32 * NH,)),
-            dma((8,)), dma((8,)), dma((4,)),
+            dma((8,)), dma((8,)),
         ],
         compiler_params=pltpu.CompilerParams(
-            collective_id=1, has_side_effects=True, vmem_limit_bytes=52 << 20
+            collective_id=1, has_side_effects=True, vmem_limit_bytes=38 << 20
         ),
         name="exchange",
-    )(pan, child_blocks, child_rows, child_cols, child_rows, child_cols, child_count)
+    )(front, child_blocks, child_rows, child_cols, child_rows, child_cols, child_count)
 
 
 def finish(mode, front_ref, recv_ref, lrh_ref, lrl_ref, lch_ref, lcl_ref, corner_ref, out_ref, add_ref, code_ref):
@@ -614,7 +623,7 @@
             return carry
         lax.fori_loop(0,16,slot,0)
     special=jnp.logical_and(i==0,r<2)
-    ah=lrh_ref[0]; al=lrl_ref[0]
+    ah=lrh_ref[i]; al=lrl_ref[i]
     for j in range(8):
         bh=lch_ref[j]; bl=lcl_ref[j]
         if "noup" in mode: u=0.0
@@ -635,18 +644,14 @@
     return pl.pallas_call(functools.partial(finish,mode),grid=(4,),
         out_shape=jax.ShapeDtypeStruct((4,256,8,256),F32),
         in_specs=[pl.BlockSpec((1,256,8,256),lambda i:(i,0,0,0)),
-                  pl.BlockSpec((16,264,256),lambda i:(0,0,0)),
-                  pl.BlockSpec((1,256,512),lambda i:(i,0,0)),pl.BlockSpec((1,256,512),lambda i:(i,0,0)),
-                  pl.BlockSpec((8,256,512),lambda i:(0,0,0)),pl.BlockSpec((8,256,512),lambda i:(0,0,0)),
-                  pl.BlockSpec((256,256),lambda i:(0,0))],
+                  *[pl.BlockSpec(memory_space=pltpu.VMEM)]*6],
         out_specs=pl.BlockSpec((1,256,8,256),lambda i:(i,0,0,0)),
         scratch_shapes=[pltpu.VMEM((8,256,256),F32),pltpu.SMEM((16,),jnp.int32)],
-        compiler_params=pltpu.CompilerParams(vmem_limit_bytes=48<<20),name="finish_"+mode.replace(" ","_"))(front,recv,lrh,lrl,lch,lcl,corner)
+        compiler_params=pltpu.CompilerParams(vmem_limit_bytes=20<<20),name="finish_"+mode.replace(" ","_"))(front,recv,lrh,lrl,lch,lcl,corner)
 
 
 def local(front, child_blocks, child_rows, child_cols, child_count):
-    pan = front[:, :, 0, :]
-    recv, lrh, lrl, lch, lcl, corner = exchange(pan, child_blocks, child_rows, child_cols, child_count)
+    recv, lrh, lrl, lch, lcl, corner = exchange(front, child_blocks, child_rows, child_cols, child_count)
     return kernel_b("", front, recv, lrh, lrl, lch, lcl, corner)
 
 

time: 127 us -> 115 us (0.906); the launches traced: 127 us -> 113 us
  Pallas kernels: 117 us -> 109 us
  local copies, waits for them, and re-layouts: 9.16 us -> 2.98 us
    pallas_call x1, Pallas kernels: 21.2 us -> 16.4 us  [kernel_b(): pl.pallas_call(functools.partial(finish, mode), grid=(4,), out_shape=jax....]
    slice x1 -> x0, local copies, waits for them, and re-layouts: 3.92 us -> none  [local(): pan = front[:, :, 0, :]]
    pallas_call x1, Pallas kernels: 95.9 us -> 93.1 us  [exchange(): pl.pallas_call(comm_kernel, out_shape=(jax.ShapeDtypeStruct((16, 264, 256...]
    unnamed x9 -> x8, local copies, waits for them, and re-layouts: 5.24 us -> 2.98 us
where the time goes in v4:
time: 115 us; the launch traced here: 113 us
  Pallas kernels  109 us (95%)
  local copies, waits for them, and re-layouts  2.98 us (3%)
    pallas_call x1, Pallas kernels, exchange(): pl.pallas_call(comm_kernel, out_shape=(jax.ShapeDtypeStruct((16, 264, 256...  93.1 us
    pallas_call x1, Pallas kernels, kernel_b(): pl.pallas_call(functools.partial(finish, mode), grid=(4,), out_shape=jax....  16.4 us
    unnamed x8, local copies, waits for them, and re-layouts  2.98 us

profile of v4, /device:TPU:11, one launch (start us, length us, event | category | flops | bytes accessed | tf_op | source)
XLA Modules:
  0.0 113.1 jit_solution(5385178048260127966)
XLA Ops:
  0.7 0.0 copy-start.1
  0.7 1.6 %copy-done.1 = f32[8,256,256]{2,1,0:T(8,128)S(1)} copy-done((f32[8,256,256]{2,1,0:T(8,128)S(1)}, f32[8,256,256]{2,1,0:T(8,128)}, u32[]{:S(2)}) %copy-start.1) | copy-done | bytes 2097176
  2.2 0.0 copy-start.2
  2.2 0.7 copy-done.2
  2.9 0.0 copy-start.3
  2.9 0.7 copy-done.3
  3.6 0.0 copy-start
  3.6 93.1 %exchange.1 = (f32[16,264,256]{2,1,0:T(8,128)S(1)}, bf16[4,256,512]{2,1,0:T(8,128)(2,1)S(1)}, bf16[4,256,512]{2,1,0:T(8,128)(2,1)S(1)}, bf16[8,256,512]{2,1,0:T(...) custom-call(f32[4,256,8,256]{3,2,1,0:T(8,128)} %front_ref.1, f32[8,256,256]{2,1,0:T(8,128)S(1)} %copy-done.1, ...), custom_call_target="tpu_custom_call" | custom-call | tf_op jit(solution)/shard_map/exchange/pallas_call | solution.py:563
  96.8 0.0 copy-done
  96.8 16.4 %finish_.1 = f32[4,256,8,256]{3,2,1,0:T(8,128)} custom-call(f32[4,256,8,256]{3,2,1,0:T(8,128)S(1)} %copy-done, f32[16,264,256]{2,1,0:T(8,128)S(1)} %get-tuple-element.11.recv_ref, bf16[4,256,512]{2,1,0:T(8,128)(2,1)S(1)} %get-tuple-element.12.lrh_ref, bf16[4,256,512]{2,1,0:T(8,128)(2,1)S(1)} %get-tuple-element.13.lrl_ref, ...), custom_call_target="tpu_custom_call" | custom-call | tf_op jit(solution)/shard_map/finish_/pallas_call | solution.py:644
Async XLA Ops:
  0.7 1.6 %copy-start.1 = (f32[8,256,256]{2,1,0:T(8,128)S(1)}, f32[8,256,256]{2,1,0:T(8,128)}, u32[]{:S(2)}) copy-start(f32[8,256,256]{2,1,0:T(8,128)} %cb_in.1) | copy-start | bytes 6291460
  2.2 0.7 copy-start.2
  2.9 0.7 copy-start.3
  3.6 93.1 %copy-start = (f32[4,256,8,256]{3,2,1,0:T(8,128)S(1)}, f32[4,256,8,256]{3,2,1,0:T(8,128)}, u32[]{:S(2)}) copy-start(f32[4,256,8,256]{3,2,1,0:T(8,128)} %front_ref.1) | copy-start | bytes 25165828

commit v5 on v4

--- a/solution.py
+++ b/solution.py
@@ -90,7 +90,6 @@
 DQ = 2
 YH = 4
 CSTEP = 4
-LAG = 1
 NH = 1
 
 
@@ -102,8 +101,8 @@
     front, cb_in, crow, ccol, crow_s, ccol_s, cnt_s,
     recv, lrh, lrl, lch, lcl, corner,
     fbuf, pan, cb, lsem,
-    stage, PR, PC, DG, AW, Wh, Wl,
-    h1, h3, h4, h5, y0s, y0r, y1s, y1r, ds, dr, dloc, xs_, xr_, cs, cr,
+    stage, PR, PC, DG, AW, W3, LR,
+    h1, h3, h4, h5, h6, y0s, y0r, y1s, y1r, ds, dr, dloc, xs_, xr_, cs, cr,
 ):
     r = lax.axis_index("row")
     c = lax.axis_index("col")
@@ -274,6 +273,50 @@
                 for cp in copies:
                     cp.start()
 
+    i0 = lax.broadcasted_iota(jnp.int32, (256, 256), 0)
+    i1 = lax.broadcasted_iota(jnp.int32, (256, 256), 1)
+    low = i1 <= i0
+    def prepare():
+        for n, w in enumerate((
+            jnp.where(low, AW[0:256, 0:256], 0.0),
+            AW[256:512, 0:256],
+            jnp.where(low, AW[256:512, 256:512], 0.0),
+        )):
+            hi, lo = split(w)
+            W3[n, :, 0:256], W3[n, :, 256:512], W3[n, :, 512:768] = hi, lo, hi
+
+    def times_w(a3, w):
+        return bdot(a3, W3[w], NT)
+
+    def solve(m0, m1, put):
+        h, l = split(m0)
+        a0 = jnp.concatenate([h, h, l], axis=1)
+        h, l = split(m1)
+        a1 = jnp.concatenate([h, h, l], axis=1)
+        put(0, times_w(a0, 0))
+        put(1, times_w(a0, 1) + times_w(a1, 2))
+
+    def row_solve(i, carry):
+        def put(p, v):
+            cols = pl.ds(p * 256, 256)
+            LR[i, :, cols] = v
+            lrh[i, :, cols], lrl[i, :, cols] = split(v)
+
+        solve(PR[2 * i], PR[2 * i + 1], put)
+        return carry
+
+
+    def col_solve(i, carry):
+        def put(p, v):
+            cols = pl.ds(p * 256, 256)
+            lch[i, :, cols], lcl[i, :, cols] = split(v)
+
+        row_set, j = k + 2 * lax.rem(i, 2), 2 * (i // 2)
+        solve(PC[row_set, j], PC[row_set, j + 1], put)
+        return carry
+
+    lr_copy = rcopy(LR, LR, h6.at[0], h6.at[1], other)
+
     @pl.when(k == 0)
     def _():
         @pl.when(y == 0)
@@ -350,13 +393,20 @@
         factor(AW)
         h3_copy.start()
 
-        def h5_wait(i, carry):
+        prepare()
+        lax.fori_loop(0, 4, row_solve, 0)
+        lr_copy.start()
+
+        def col_pair(br, carry):
+            for i in range(2):
+                for src in range(2):
+                    for h in range(NH):
+                        h5_copy(2 * br + i, src, h).wait_recv()
             for src in range(2):
-                for h in range(NH):
-                    h5_copy(i, src, h).wait_recv()
-            return carry
-
-        lax.fori_loop(0, 8, h5_wait, 0)
+                col_solve(2 * br + src, 0)
+            return carry
+
+        lax.fori_loop(0, 4, col_pair, 0)
 
     xz_off = []
     xz_depth = []
@@ -394,7 +444,7 @@
             for h in range(NH):
                 for s in range(4):
                     dep = xz_depth[s]
-                    i = t - LAG * dep
+                    i = t - dep
 
                     @pl.when(jnp.logical_and(i >= 0, i < 8))
                     def _(s=s, dep=dep, i=i, h=h):
@@ -422,7 +472,11 @@
 
         lax.fori_loop(0, CSTEP, xz_step, 0)
         start_children()
-        lax.fori_loop(CSTEP, 8 + 4 * LAG, xz_step, 0)
+        lax.fori_loop(CSTEP, 11, xz_step, 0)
+        h3_copy.wait_recv()
+        prepare()
+        lax.fori_loop(0, 4, col_solve, 0)
+        lax.fori_loop(11, 12, xz_step, 0)
 
         def h4_wait(j, carry):
             h4_copy(j).wait_recv()
@@ -432,46 +486,11 @@
         def _():
             lax.fori_loop(0, 8, h4_wait, 0)
 
-        h3_copy.wait_recv()
-
-    i0 = lax.broadcasted_iota(jnp.int32, (256, 256), 0)
-    i1 = lax.broadcasted_iota(jnp.int32, (256, 256), 1)
-    low = i1 <= i0
-    Wh[0], Wl[0] = split(jnp.where(low, AW[0:256, 0:256], 0.0))
-    Wh[1], Wl[1] = split(AW[256:512, 0:256])
-    Wh[2], Wl[2] = split(jnp.where(low, AW[256:512, 256:512], 0.0))
-
-    def times_w(h, l, w):
-        return bdot(h, Wh[w], NT) + (bdot(h, Wl[w], NT) + bdot(l, Wh[w], NT))
-
-    def solve(m0, m1, put):
-        h0_, l0_ = split(m0)
-        h1_, l1_ = split(m1)
-        a = times_w(h0_, l0_, 0)
-        put(0, *split(a))
-        e = times_w(h0_, l0_, 1) + times_w(h1_, l1_, 2)
-        put(1, *split(e))
-
-    def row_solve(i, carry):
-        def put(p, hi, lo):
-            lrh[i, :, pl.ds(p * 256, 256)] = hi
-            lrl[i, :, pl.ds(p * 256, 256)] = lo
-
-        solve(PR[2 * i], PR[2 * i + 1], put)
-        return carry
-
-    lax.fori_loop(0, 4, row_solve, 0)
-
-    def col_solve(i, carry):
-        def put(p, hi, lo):
-            lch[i, :, pl.ds(p * 256, 256)] = hi
-            lcl[i, :, pl.ds(p * 256, 256)] = lo
-
-        row_set, j = k + 2 * lax.rem(i, 2), 2 * (i // 2)
-        solve(PC[row_set, j], PC[row_set, j + 1], put)
-        return carry
-
-    lax.fori_loop(0, 8, col_solve, 0)
+        lax.fori_loop(4, 8, col_solve, 0)
+        lr_copy.wait_recv()
+        for i in range(4):
+            lrh[i], lrl[i] = split(LR[i])
+
     corner[...] = jnp.zeros((256, 256), F32)
 
     def diag_block(o):
@@ -528,6 +547,7 @@
                     cp.wait_send()
 
         h3_copy.wait_send()
+        lr_copy.wait_send()
 
     @pl.when(k == 1)
     def _():
@@ -582,9 +602,9 @@
             pltpu.VMEM((4, 8, 256, 256), F32),
             pltpu.VMEM((3, 256, 256), F32),
             pltpu.VMEM((512, 512), F32),
-            pltpu.VMEM((3, 256, 256), BF),
-            pltpu.VMEM((3, 256, 256), BF),
-            dma((4, 2)), dma((2,)), dma((8, 2)), dma((16 * NH, 2)),
+            pltpu.VMEM((3, 256, 768), BF),
+            pltpu.VMEM((4, 256, 512), F32),
+            dma((4, 2)), dma((2,)), dma((8, 2)), dma((16 * NH, 2)), dma((2,)),
             dma((8, 2)), dma((8,)), dma((8 * YH,)), dma((8 * YH,)),
             dma((12, 4)), dma((12,)), dma, dma((32 * NH, 4)), dma((32 * NH,)),
             dma((8,)), dma((8,)),
@@ -596,7 +616,7 @@
     )(front, child_blocks, child_rows, child_cols, child_rows, child_cols, child_count)
 
 
-def finish(mode, front_ref, recv_ref, lrh_ref, lrl_ref, lch_ref, lcl_ref, corner_ref, out_ref, add_ref, code_ref):
+def finish(mode, front_ref, recv_ref, lrh_ref, lrl_ref, lch_ref, lcl_ref, corner_ref, out_ref, code_ref):
     i=pl.program_id(0)
     r=lax.axis_index("row") if "nomesh" not in mode else 3
     c=lax.axis_index("col") if "nomesh" not in mode else 3
@@ -604,7 +624,13 @@
     def _():
         for s in range(16):
             code_ref[s]=jnp.max(recv_ref[s,258:259,:]).astype(jnp.int32)
-    add_ref[...]=jnp.zeros_like(add_ref)
+    special=jnp.logical_and(i==0,r<2)
+    ah=lrh_ref[i]; al=lrl_ref[i]
+    a3=jnp.concatenate([ah,ah,al],axis=1)
+    for j in range(8):
+        bh=lch_ref[j]; bl=lcl_ref[j]
+        u=bdot(a3,jnp.concatenate([bh,bl,bh],axis=1),NT)
+        out_ref[0,:,j,:]=front_ref[0,:,j,:]-u
     if "noch" not in mode:
         def slot(s,carry):
             code=code_ref[s]
@@ -618,18 +644,13 @@
                 h,l=split(recv_ref[s,0:256,:])
                 p=bdot(R,h,NN)+bdot(R,l,NN)
                 h,l=split(p)
-                j=code&7
-                add_ref[j]=add_ref[j]+(bdot(h,Q,NT)+bdot(l,Q,NT))
+                p=bdot(h,Q,NT)+bdot(l,Q,NT)
+                for j in range(8):
+                    @pl.when((code&7)==j)
+                    def _(j=j):
+                        out_ref[0,:,j,:]=out_ref[0,:,j,:]+p
             return carry
         lax.fori_loop(0,16,slot,0)
-    special=jnp.logical_and(i==0,r<2)
-    ah=lrh_ref[i]; al=lrl_ref[i]
-    for j in range(8):
-        bh=lch_ref[j]; bl=lcl_ref[j]
-        if "noup" in mode: u=0.0
-        else: u=bdot(ah,bh,NT)+(bdot(ah,bl,NT)+bdot(al,bh,NT))
-        v=front_ref[0,:,j,:]+add_ref[j]-u
-        out_ref[0,:,j,:]=v
     @pl.when(c<2)
     def _():
         @pl.when(c==0)
@@ -646,7 +667,7 @@
         in_specs=[pl.BlockSpec((1,256,8,256),lambda i:(i,0,0,0)),
                   *[pl.BlockSpec(memory_space=pltpu.VMEM)]*6],
         out_specs=pl.BlockSpec((1,256,8,256),lambda i:(i,0,0,0)),
-        scratch_shapes=[pltpu.VMEM((8,256,256),F32),pltpu.SMEM((16,),jnp.int32)],
+        scratch_shapes=[pltpu.SMEM((16,),jnp.int32)],
         compiler_params=pltpu.CompilerParams(vmem_limit_bytes=20<<20),name="finish_"+mode.replace(" ","_"))(front,recv,lrh,lrl,lch,lcl,corner)
 
 

time: 115 us -> 113 us (0.983)
  the two profiles are of different devices: /device:TPU:11 before, /device:TPU:37 now
where the time goes in v5:
time: 113 us
  Pallas kernels  109 us (96%)
  local copies, waits for them, and re-layouts  2.98 us (3%)
    pallas_call x1, Pallas kernels, exchange(): pl.pallas_call(comm_kernel, out_shape=(jax.ShapeDtypeStruct((16, 264, 256...  90 us
    pallas_call x1, Pallas kernels, kernel_b(): pl.pallas_call(functools.partial(finish, mode), grid=(4,), out_shape=jax....  18.9 us
    unnamed x8, local copies, waits for them, and re-layouts  2.98 us

profile of v5, /device:TPU:37, one launch (start us, length us, event | category | flops | bytes accessed | tf_op | source)
XLA Modules:
  0.0 112.6 jit_solution(5444427313579962755)
XLA Ops:
  0.7 0.0 copy-start.1
  0.7 1.6 %copy-done.1 = f32[8,256,256]{2,1,0:T(8,128)S(1)} copy-done((f32[8,256,256]{2,1,0:T(8,128)S(1)}, f32[8,256,256]{2,1,0:T(8,128)}, u32[]{:S(2)}) %copy-start.1) | copy-done | bytes 2097176
  2.2 0.0 copy-start.2
  2.2 0.7 copy-done.2
  2.9 0.0 copy-start.3
  2.9 0.7 copy-done.3
  3.6 0.0 copy-start
  3.6 90.0 %exchange.1 = (f32[16,264,256]{2,1,0:T(8,128)S(1)}, bf16[4,256,512]{2,1,0:T(8,128)(2,1)S(1)}, bf16[4,256,512]{2,1,0:T(8,128)(2,1)S(1)}, bf16[8,256,512]{2,1,0:T(...) custom-call(f32[4,256,8,256]{3,2,1,0:T(8,128)} %front_ref.1, f32[8,256,256]{2,1,0:T(8,128)S(1)} %copy-done.1, ...), custom_call_target="tpu_custom_call" | custom-call | tf_op jit(solution)/shard_map/exchange/pallas_call | solution.py:583
  93.7 0.0 copy-done
  93.7 18.9 %finish_.1 = f32[4,256,8,256]{3,2,1,0:T(8,128)} custom-call(f32[4,256,8,256]{3,2,1,0:T(8,128)S(1)} %copy-done, f32[16,264,256]{2,1,0:T(8,128)S(1)} %get-tuple-element.11.recv_ref, bf16[4,256,512]{2,1,0:T(8,128)(2,1)S(1)} %get-tuple-element.12.lrh_ref, bf16[4,256,512]{2,1,0:T(8,128)(2,1)S(1)} %get-tuple-element.13.lrl_ref, ...), custom_call_target="tpu_custom_call" | custom-call | tf_op jit(solution)/shard_map/finish_/pallas_call | solution.py:665
Async XLA Ops:
  0.7 1.6 %copy-start.1 = (f32[8,256,256]{2,1,0:T(8,128)S(1)}, f32[8,256,256]{2,1,0:T(8,128)}, u32[]{:S(2)}) copy-start(f32[8,256,256]{2,1,0:T(8,128)} %cb_in.1) | copy-start | bytes 6291460
  2.2 0.7 copy-start.2
  2.9 0.7 copy-start.3
  3.6 90.0 %copy-start = (f32[4,256,8,256]{3,2,1,0:T(8,128)S(1)}, f32[4,256,8,256]{3,2,1,0:T(8,128)}, u32[]{:S(2)}) copy-start(f32[4,256,8,256]{3,2,1,0:T(8,128)} %front_ref.1) | copy-start | bytes 25165828
